TPU v7x, 32 devices: a whole 2x2x4 slice. The times are simulated.
32 devices in a mesh: ctx: 8 (over z, x), grp: 4 (over y, core).
Axes of the slice: x: 2, y: 2, z: 4, core: 2. Of those that a mesh axis runs over, the one named last changes fastest.
Arguments:
- query_heads: bfloat16 [4096, 2048], P('ctx', 'grp'), may hold values from -6 to 6
- key_heads: bfloat16 [4096, 2048], P('ctx', 'grp'), may hold values from -6 to 6
- value_heads: bfloat16 [4096, 2048], P('ctx', 'grp'), may hold values from -6 to 6
- log_decay: float32 [16, 4096], P('grp', 'ctx'), may hold values from -1 to 0
- residual: bfloat16 [4096, 2048], P(('ctx', 'grp')), may hold values from -4 to 4
- out_weight: bfloat16 [2048, 2048], replicated, may hold values from -0.5 to 0.5
- norm_gain: float32 [2048], replicated, may hold values from 0.25 to 1.75
- expert_ids: int32 [4096, 6], P(('ctx', 'grp')), may hold values from 0 to 63, all different within a row; in each aligned block of 128 rows (0 to 127, 128 to 255, ...) at most 15 rows name the same one
- gate_weights: float32 [4096, 6], P(('ctx', 'grp')), may hold values from 0.1 to 1
- gate_proj: bfloat16 [64, 2048, 1408], P('ctx', None, 'grp'), may hold values from -0.125 to 0.125
- up_proj: bfloat16 [64, 2048, 1408], P('ctx', None, 'grp'), may hold values from -0.125 to 0.125
- down_proj: bfloat16 [64, 1408, 2048], P('ctx', 'grp'), may hold values from -0.15625 to 0.15625
Outputs:
- attended: bfloat16 [4096, 2048], P(('ctx', 'grp'))
- layer_out: bfloat16 [4096, 2048], P(('ctx', 'grp'))
Inputs may be any that keep to these rules, and one draw needn't show every extreme that they name: `expert_ids`: each token names 6 different experts. In each aligned block of 128 tokens no expert is named by more than 15 tokens, and that bound is reached.
All inputs are finite; a program needn't handle non-finite values.
Results may differ from a plain program's by a relative error of at most 0.02.
Values may be sent and summed in bfloat16 or wider, within the bound.
A program may use at most 128 MiB of HBM per device.

v0:
```python
import jax
import jax.numpy as jnp
from jax import lax
from jax.sharding import PartitionSpec as P

D = 2048
HD = 128
E = 64
TOPK = 6


def entering(array, axis, combine, identity):
    count, index = (lax.axis_size(axis), lax.axis_index(axis))
    everything = jax.tree.map(
        lambda part, kind: lax.all_gather(part.astype(kind), axis),
        array,
        (jnp.bfloat16, jnp.bfloat16, jnp.bfloat16),
    )
    start = jax.tree.map(
        lambda part, zero: jnp.broadcast_to(jnp.asarray(zero, part.dtype), part.shape),
        array,
        identity,
    )

    def lap(k, before):
        reached = k < index
        new = combine(
            before, jax.tree.map(lambda part, own: part[k].astype(own.dtype), everything, array)
        )
        return jax.tree.map(lambda a, b: jnp.where(reached, a, b), new, before)

    return lax.fori_loop(0, count, lap, start)


def feature_map(values):
    return (jax.nn.elu(values.astype(jnp.float32)) + 1.0).astype(jnp.bfloat16)


def summarize(feat_key, value_rows, log_decay):
    cumulative = jnp.cumsum(log_decay, axis=1)
    block_total = cumulative[:, -1]
    trailing_keys = (
        feat_key.astype(jnp.float32) * jnp.exp(block_total[:, None] - cumulative).T[:, :, None]
    )
    shard_state = jnp.einsum(
        "jfi,jfx->fix",
        trailing_keys.astype(jnp.bfloat16),
        value_rows,
        preferred_element_type=jnp.float32,
    )
    local_norm = jnp.sum(trailing_keys, axis=0)
    return (cumulative, block_total, shard_state, local_norm)


def block_output(feat_query, feat_key, value_rows, cumulative, preceding_state, prior_norm):
    length = feat_query.shape[0]
    scores = jnp.einsum("thd,shd->hts", feat_query, feat_key, preferred_element_type=jnp.float32)
    row_index = lax.broadcasted_iota(jnp.int32, (length, length), 0)
    col_index = lax.broadcasted_iota(jnp.int32, (length, length), 1)
    causal = (col_index <= row_index)[None]
    spread = cumulative[:, :, None] - cumulative[:, None, :]
    weights = jnp.where(causal, scores * jnp.exp(jnp.where(causal, spread, 0.0)), 0.0)
    inner_den = jnp.sum(weights, axis=2).T
    inner_num = jnp.einsum(
        "hts,shd->thd", weights.astype(jnp.bfloat16), value_rows, preferred_element_type=jnp.float32
    )
    query_damping = feat_query.astype(jnp.float32) * jnp.exp(cumulative).T[:, :, None]
    outer_numerator = jnp.einsum(
        "cnm,nmp->cnp", query_damping, preceding_state, precision=lax.Precision.HIGHEST
    )
    outer_den = jnp.einsum("thk,hk->th", query_damping, prior_norm, precision=lax.Precision.HIGHEST)
    mixed_rows = ((inner_num + outer_numerator) / (inner_den + outer_den)[:, :, None]).astype(
        jnp.bfloat16
    )
    return mixed_rows.reshape(length, -1)


def merge_states(earlier_part, later_part):
    first_total, first_state, first_norm = earlier_part
    second_total, second_state, second_norm = later_part
    factor = jnp.exp(second_total)
    return (
        first_total + second_total,
        factor[:, None, None] * first_state + second_state,
        factor[:, None] * first_norm + second_norm,
    )


def route_tokens(expert_ids, gate_weights, normed, capacity):
    row_count = expert_ids.shape[0]
    onehot = (expert_ids[:, :, None] == jnp.arange(E, dtype=jnp.int32)).astype(jnp.int32)
    flat_hits = onehot.reshape(row_count * TOPK, E)
    earlier = jnp.cumsum(flat_hits, axis=0) - flat_hits
    slot_index = jnp.sum(earlier * flat_hits, axis=1).reshape(row_count, TOPK)
    target = expert_ids * capacity + slot_index
    placed = (target[:, :, None] == jnp.arange(E * capacity, dtype=jnp.int32)).astype(jnp.float32)
    dispatch_rows = jnp.sum(placed, axis=1).astype(jnp.bfloat16)
    combiner = jnp.sum(
        placed * gate_weights.astype(jnp.bfloat16).astype(jnp.float32)[:, :, None], axis=1
    ).astype(jnp.bfloat16)
    buffer = jnp.einsum(
        "rs,rd->sd", dispatch_rows, normed, preferred_element_type=jnp.float32
    ).astype(jnp.bfloat16)
    return (buffer, combiner)


def on_device(
    query_heads,
    key_heads,
    value_heads,
    log_decay,
    residual,
    out_weight,
    norm_gain,
    expert_ids,
    gate_weights,
    gate_proj,
    up_proj,
    down_proj,
):
    length = query_heads.shape[0]
    local_heads = query_heads.shape[1] // HD
    feat_query = feature_map(query_heads).reshape(length, local_heads, HD)
    feat_key = feature_map(key_heads).reshape(length, local_heads, HD)
    value_rows = value_heads.reshape(length, local_heads, HD)
    cumulative, block_total, shard_state, local_norm = summarize(feat_key, value_rows, log_decay)
    start_state = (
        jnp.zeros_like(block_total),
        jnp.zeros_like(shard_state),
        jnp.zeros_like(local_norm),
    )
    _, preceding_state, prior_norm = entering(
        (block_total, shard_state, local_norm), "ctx", merge_states, start_state
    )
    mixed_rows = block_output(
        feat_query, feat_key, value_rows, cumulative, preceding_state, prior_norm
    )
    head_rows = lax.all_to_all(mixed_rows, "grp", split_axis=0, concat_axis=1, tiled=True)
    projected = jnp.dot(head_rows, out_weight, preferred_element_type=jnp.float32)
    attended = (residual.astype(jnp.float32) + projected).astype(jnp.bfloat16)
    widened = attended.astype(jnp.float32)
    normed = (
        widened * lax.rsqrt(jnp.mean(widened * widened, axis=1, keepdims=True) + 1e-06) * norm_gain
    ).astype(jnp.bfloat16)
    row_count = expert_ids.shape[0]
    capacity = (5 * row_count * TOPK + 4 * E - 1) // (4 * E)
    buffer, combiner = route_tokens(expert_ids, gate_weights, normed, capacity)
    ctx_count = lax.axis_size("ctx")
    local_experts = gate_proj.shape[0]
    outgoing = buffer.reshape(ctx_count, local_experts, capacity, D)
    arrived = lax.all_to_all(outgoing, "ctx", split_axis=0, concat_axis=0, tiled=True)
    block_rows = lax.all_gather(arrived, "grp", axis=0, tiled=True)
    gate_part = jnp.einsum(
        "secd,edf->secf", block_rows, gate_proj, preferred_element_type=jnp.float32
    )
    up_part = jnp.einsum("secd,edf->secf", block_rows, up_proj, preferred_element_type=jnp.float32)
    hidden = (jax.nn.silu(gate_part) * up_part).astype(jnp.bfloat16)
    partial_out = jnp.einsum(
        "secf,efd->secd", hidden, down_proj, preferred_element_type=jnp.float32
    ).astype(jnp.bfloat16)
    summed = lax.psum_scatter(
        partial_out.astype(jnp.float32).astype(jnp.bfloat16), "grp", scatter_dimension=0, tiled=True
    )
    returned = lax.all_to_all(summed, "ctx", split_axis=0, concat_axis=0, tiled=True)
    expert_mix = jnp.dot(combiner, returned.reshape(-1, D), preferred_element_type=jnp.float32)
    layer_out = (widened + expert_mix).astype(jnp.bfloat16)
    return (attended, layer_out)


def solution(mesh):
    placed = (
        P("ctx", "grp"),
        P("ctx", "grp"),
        P("ctx", "grp"),
        P("grp", "ctx"),
        P(("ctx", "grp"), None),
        P(),
        P(),
        P(("ctx", "grp"), None),
        P(("ctx", "grp"), None),
        P("ctx", None, "grp"),
        P("ctx", None, "grp"),
        P("ctx", "grp", None),
    )
    return jax.shard_map(
        on_device,
        mesh=mesh,
        in_specs=placed,
        out_specs=(P(("ctx", "grp"), None), P(("ctx", "grp"), None)),
        check_vma=False,
    )
```

profile of v0, /device:TPU:0, one launch (start us, length us, event | category | flops | bytes accessed | tf_op | source)
XLA Modules:
  0.0 617.0 jit_solution(8112946582527675623)
XLA Ops:
  7.2 0.8 reshape.149
  8.0 1.2 reduce-window.14
  10.0 0.3 copy.145
  10.4 1.6 multiply_reduce_fusion
  12.2 1.0 convolution_convert_fusion.1
  13.2 0.6 dynamic-slice
  14.5 0.2 dynamic-update-slice
  14.7 23.1 %all-reduce = bf16[32]{0:T(256)(128)(2,1)S(1)} all-reduce(bf16[32]{0:T(256)(128)(2,1)S(1)} %dynamic-update-slice), channel_id=2, replica_groups=mesh['ctx'=8,'grp'=4] {'ctx'}, use_global_device_ids=true, to_apply=%add | all-reduce | flops 32 | bytes 128
  38.3 1.8 reduce-window.16
  40.1 0.3 slice_reduce_fusion
  40.8 16.3 %all_gather.20 = bf16[8,4,128]{2,1,0:T(4,128)(2,1)S(1)} all-gather(bf16[1,4,128]{2,1,0:T(4,128)(2,1)S(1)} %bitcast.179), channel_id=1, replica_groups=mesh['ctx'=8,'grp'=4] {'ctx'}, dimensions={0}, use_global_device_ids=true | all-gather | bytes 9216 | tf_op jit(solution)/shard_map/all_gather | solution.py:15
  57.2 1.9 fusion.16
  59.1 2.7 fusion.25
  61.8 9.0 %while.16 = (s32[]{:T(128)}, f32[4,128,128]{2,1,0:T(8,128)S(1)}, f32[4,128]{1,0:T(4,128)S(1)}, s32[]{:T(128)}, bf16[8,4]{1,0:T(8,128)(2,1)S(1)}, /*index=5*/bf16...) while((s32[]{:T(128)}, f32[4,128,128]{2,1,0:T(8,128)S(1)}, ...), condition=%wide.region_4.5_spmd.clone, body=%wide.region_3.4_spmd.clone.sunk | while | flops 330248 | bytes 660671 | solution.py:32
  61.9 1.0 fusion.90
  63.1 1.0 fusion.90
  64.2 1.0 fusion.90
  65.3 1.0 fusion.90
  66.5 1.0 fusion.90
  67.6 1.0 fusion.90
  68.7 1.0 fusion.90
  69.9 1.0 fusion.90
  70.9 1.4 fusion.40
  72.3 2.7 fusion.30
  75.1 0.4 copy.127
  75.5 1.0 all_to_all.20
  76.5 3.5 all-to-all-start
  80.2 0.6 select_reduce_fusion
  80.9 7.9 %all-to-all-done = bf16[4,128,512]{2,1,0:T(8,128)(2,1)S(1)} async-done(((bf16[4,128,512]{2,1,0:T(8,128)(2,1)}), bf16[4,128,512]{2,1,0:T(8,128)(2,1)S(1)}, u32[]{:S(2)}, u32[]{:S(2)}) %all-to-all-start) | async-done | bytes 524320 | tf_op jit(solution)/shard_map/all_to_all | solution.py:138
  88.8 0.3 copy.128
  89.1 4.8 fusion.31
  93.9 3.1 convolution_convert_fusion
  97.0 5.1 reshape.154
  102.2 4.6 copy.133
  106.7 90.7 %all_to_all.29 = bf16[8,8,15,2048]{3,1,2,0:T(8,128)(2,1)S(1)} all-to-all(bf16[8,8,15,2048]{3,1,2,0:T(8,128)(2,1)S(1)} %copy.133), channel_id=1, replica_groups=mesh['ctx'=8,'grp'=4] {'ctx'}, dimensions={0} | all-to-all | bytes 7864320 | tf_op jit(solution)/shard_map/all_to_all | solution.py:151
  197.4 4.0 copy.134
  201.5 0.3 reduce-scatter.4.cloned.1.call-start
  201.8 97.8 %all-gather.5.cloned.1.call-done = bf16[32,8,15,2048]{3,0,2,1:T(8,128)(2,1)} async-done(((bf16[8,8,15,2048]{3,0,2,1:T(8,128)(2,1)}), bf16[32,8,15,2048]{3,0,2,1:T(8,128)(2,1)}) %all-gather.5.cloned.1.call-update) | async-done | bytes 15728656 | tf_op jit(solution)/shard_map/all_gather | solution.py:152
  299.6 16.9 %fusion.6 = f32[8,32,15,352]{3,1,2,0:T(8,128)} fusion(bf16[32,8,15,2048]{3,0,2,1:T(8,128)(2,1)} %all-gather.5.cloned.1.call-done, bf16[8,2048,352]{1,2,0:T(8,128)(2,1)} %param.24), kind=kOutput, calls=%fused_computation.10 | convolution fusion | flops 5536481280 | bytes 32669696 | tf_op jit(solution)/shard_map/secd,edf->secf/dot_general | solution.py:156
  316.5 25.5 %convert_bitcast_fusion = bf16[32,8,15,2048]{3,0,2,1:T(8,128)(2,1)} fusion(bf16[8,352,2048]{2,1,0:T(8,128)(2,1)} %param.25, f32[8,32,15,352]{3,1,2,0:T(8,128)} %fusion.6, bf16[32,8,15,2048]{3,0,2,1:T(8,128)(2,1)} %all-gather.5.cloned.1.call-done, bf16[8,2048,352]{1,2,0:T(8,128)(2,1)} %param.23), kind=kOutput, calls=%fused_computation.8 | convolution fusion | flops 11088936960 | bytes 59932672 | tf_op jit(solution)/shard_map/secf,efd->secd/dot_general | solution.py:158
  342.1 18.2 %copy.146 = bf16[32,8,15,2048]{3,2,1,0:T(8,128)(2,1)} copy(bf16[32,8,15,2048]{3,0,2,1:T(8,128)(2,1)} %convert_bitcast_fusion) | data formatting | bytes 31457280
  360.2 19.6 %reshape.173 = bf16[32,245760]{1,0:T(8,128)(2,1)} reshape(bf16[32,8,15,2048]{3,2,1,0:T(8,128)(2,1)} %copy.146) | data formatting | bytes 31457280
  379.8 120.0 %reduce-scatter.4.cloned.1.call-done = bf16[8,245760]{1,0:T(8,128)(2,1)} async-done(((bf16[32,245760]{1,0:T(8,128)(2,1)}), bf16[8,245760]{1,0:T(8,128)(2,1)}) %reduce-scatter.4.cloned.1.call-update) | async-done | bytes 3932176
  499.8 4.3 copy.135
  504.1 92.9 %all_to_all.30 = bf16[8,8,15,2048]{3,1,2,0:T(8,128)(2,1)S(1)} all-to-all(bf16[8,8,15,2048]{3,1,2,0:T(8,128)(2,1)S(1)} %copy.135), channel_id=1, replica_groups=mesh['ctx'=8,'grp'=4] {'ctx'}, dimensions={0} | all-to-all | bytes 7864320 | tf_op jit(solution)/shard_map/all_to_all | solution.py:164
  597.0 4.2 copy.136
  601.2 5.2 reshape.155
  606.4 3.6 fusion.19
  (67 shorter events, 3.1 us)
Async XLA Ops:
  7.2 5.0 copy-start
  7.2 6.0 copy-start.8
  7.2 30.6 %copy-start.4 = (s32[128,6]{0,1:T(8,128)S(1)}, s32[128,6]{0,1:T(8,128)}, u32[]{:S(2)}) copy-start(s32[128,6]{0,1:T(8,128)} %param.21) | copy-start | bytes 9220
  7.2 54.6 %all-gather.7.cloned.1.call-start = ((), (), s32[]{:S(2)}) async-start(), calls=%async_computation.5 | async-start | bytes 1179648 | tf_op jit(solution)/shard_map/all_gather | solution.py:15
  10.0 47.1 %copy-start.7 = (bf16[512,512]{1,0:T(8,128)(2,1)S(1)}, bf16[512,512]{1,0:T(8,128)(2,1)}, u32[]{:S(2)}) copy-start(bf16[512,512]{1,0:T(8,128)(2,1)} %param.14) | copy-start | bytes 1572868
  72.3 7.9 %copy-start.6 = (f32[128,6]{0,1:T(8,128)S(1)}, f32[128,6]{0,1:T(8,128)}, u32[]{:S(2)}) copy-start(f32[128,6]{0,1:T(8,128)} %param.22) | copy-start | bytes 9220
  72.3 16.7 %copy-start.3 = (bf16[128,2048]{1,0:T(8,128)(2,1)S(1)}, bf16[128,2048]{1,0:T(8,128)(2,1)}, u32[]{:S(2)}) copy-start(bf16[128,2048]{1,0:T(8,128)(2,1)} %param.18) | copy-start | bytes 1572868
  76.5 12.3 %all-to-all-start = ((bf16[4,128,512]{2,1,0:T(8,128)(2,1)}), bf16[4,128,512]{2,1,0:T(8,128)(2,1)S(1)}, u32[]{:S(2)}, u32[]{:S(2)}) async-start(bf16[4,128,512]{2,1,0:T(8,128)(2,1)} %all_to_all.20), calls=%async_computation | async-start | bytes 1048576 | tf_op jit(solution)/shard_map/all_to_all | solution.py:138
  80.0 219.6 %all-gather.5.cloned.1.call-start = ((), (), s32[]{:S(2)}) async-start(), calls=%async_computation.4 | async-start | bytes 19660800 | tf_op jit(solution)/shard_map/all_gather | solution.py:152
  89.1 4.8 copy-start.5
  93.9 512.5 %copy-start.2 = (bf16[128,2048]{1,0:T(8,128)(2,1)}, bf16[128,2048]{1,0:T(8,128)(2,1)S(1)}, u32[]{:S(2)}) copy-start(bf16[128,2048]{1,0:T(8,128)(2,1)S(1)} %get-tuple-element.176) | copy-start | bytes 1572868
  201.5 298.3 %reduce-scatter.4.cloned.1.call-start = ((), (), s32[]{:S(2)}) async-start(), calls=%async_computation.6 | async-start | bytes 19660800
  601.2 8.8 %copy-start.1 = (bf16[512,512]{1,0:T(8,128)(2,1)S(1)}, bf16[512,512]{1,0:T(8,128)(2,1)}, u32[]{:S(2)}) copy-start(bf16[512,512]{1,0:T(8,128)(2,1)} %param.16) | copy-start | bytes 1572868
Sparse Core Ops, SparseCore 0:
  13.3 43.0 all-gather.6
  201.6 97.9 all-gather.4
  380.0 119.8 reduce-scatter.3
where the time goes:
time: 625 us; the launch traced here: 617 us
  waiting for transfers between devices  226 us (36%)
  blocking collectives  223 us (36%)
  local copies, waits for them, and re-layouts  70.4 us (11%)
  matrix products  63.8 us (10%)
  between operations  15.1 us (2%)
  other arithmetic  14.7 us (2%)
    unnamed x4, waiting for transfers between devices  120 us
    all_gather x1, waiting for transfers between devices, on_device(): block_rows = lax.all_gather(arrived, 'grp', axis=0, tiled=True)  97.8 us
    all_to_all x1, blocking collectives, on_device(): lax.all_to_all(summed, 'ctx', split_axis=0, concat_axis=0, tiled=True)  92.9 us
    all_to_all x1, blocking collectives, on_device(): lax.all_to_all(outgoing, 'ctx', split_axis=0, concat_axis=0, tiled=True)  90.7 us
    unnamed x26, local copies, waits for them, and re-layouts  38.8 us
    dot_general x1, matrix products, on_device(): jnp.einsum('secf,efd->secd', hidden, down_proj, preferred_element_type=jn...  25.5 us
    unnamed x1, blocking collectives  23.1 us
    dot_general x1, matrix products, on_device(): jnp.einsum('secd,edf->secf', block_rows, up_proj, preferred_element_type=...  16.9 us
  transfers between devices with their start and end apart: 4, of which 3 were waited for; matrix products, arithmetic and copies ran while one was open for 1% of the time, Pallas kernels for 0%

commit v1 on v0

--- a/solution.py
+++ b/solution.py
@@ -1,12 +1,344 @@
+import functools
+
 import jax
 import jax.numpy as jnp
 from jax import lax
+from jax.experimental import pallas as pl
+from jax.experimental.pallas import tpu as pltpu
 from jax.sharding import PartitionSpec as P
 
 D = 2048
 HD = 128
 E = 64
 TOPK = 6
+
+
+MESH = pl.DeviceIdType.MESH
+VMEM_TOKENS = 4096
+
+
+class Grid:
+    def __init__(self, nz):
+        ctx, grp = lax.axis_index("ctx"), lax.axis_index("grp")
+        self.nz = nz
+        self.z, self.x = ctx // 2, ctx % 2
+        self.y, self.c = grp // 2, grp % 2
+        self.fx, self.fy, self.fc = 1 - self.x, 1 - self.y, 1 - self.c
+
+    def turn(self, dz):
+        return lax.rem(self.z + dz, self.nz)
+
+    def meet(self):
+        barrier = pltpu.get_barrier_semaphore()
+        partners = [device(self.turn(dz), self.x, self.y, self.c) for dz in range(1, self.nz)]
+        partners += [
+            device(self.z, self.fx, self.y, self.c),
+            device(self.z, self.x, self.fy, self.c),
+            device(self.z, self.x, self.y, self.fc),
+        ]
+        for partner in partners:
+            pl.semaphore_signal(barrier, inc=1, device_id=partner, device_id_type=MESH)
+        pl.semaphore_wait(barrier, len(partners))
+
+
+def device(z, x, y, c):
+    return (z * 2 + x, y * 2 + c)
+
+
+def block_at(z, x, y, c):
+    return (z * 2 + x) * 4 + y * 2 + c
+
+
+def gather_kernel(nz, own_ref, out_ref, send_sem, recv_sem, core_sem, local_sem):
+    at = Grid(nz)
+    half = own_ref.shape[0] // 2
+    at.meet()
+    sends = []
+
+    def send(src, dst, sem, to):
+        copy = pltpu.make_async_remote_copy(
+            src_ref=src,
+            dst_ref=dst,
+            send_sem=send_sem.at[len(sends)],
+            recv_sem=sem,
+            device_id=to,
+            device_id_type=MESH,
+        )
+        copy.start()
+        sends.append(copy)
+
+    def rows_of(z, x, y, c, h):
+        block = out_ref.at[block_at(z, x, y, c)]
+        return block if h is None else block.at[pl.ds(h * half, half)]
+
+    def sem_of(sems, z, x, y, h):
+        return sems.at[((z * 2 + x) * 2 + y) * 2 + (0 if h is None else h)]
+
+    def forward(z, x, y, h, to, src=None):
+        ref = rows_of(z, x, y, at.c, h)
+        send(ref if src is None else src, ref, sem_of(recv_sem, z, x, y, h), to)
+
+    def forward_core(z, x, y, h, src=None):
+        ref = rows_of(z, x, y, at.c, h)
+        send(
+            ref if src is None else src,
+            ref,
+            sem_of(core_sem, z, x, y, h),
+            device(at.z, at.x, at.y, at.fc),
+        )
+
+    def arrive(sems, z, x, y, c, h):
+        ref = rows_of(z, x, y, c, h)
+        pltpu.make_async_copy(ref, ref, sem_of(sems, z, x, y, h)).wait()
+
+    local = pltpu.make_async_copy(own_ref, out_ref.at[block_at(at.z, at.x, at.y, at.c)], local_sem)
+    local.start()
+    for dz in range(1, nz):
+        forward(at.z, at.x, at.y, None, device(at.turn(dz), at.x, at.y, at.c), own_ref)
+
+    to_x = device(at.z, at.fx, at.y, at.c)
+    to_y = device(at.z, at.x, at.fy, at.c)
+
+    def column(dz):
+        z = at.turn(dz)
+        if dz:
+            arrive(recv_sem, z, at.x, at.y, at.c, None)
+        src = None if dz else own_ref
+        forward(z, at.x, at.y, None, to_x, src)
+        forward(z, at.x, at.y, None, to_y, src)
+        forward_core(z, at.x, at.y, None, src)
+
+    def turned(dz):
+        z = at.turn(dz)
+        arrive(recv_sem, z, at.fx, at.y, at.c, None)
+        forward(z, at.fx, at.y, 0, to_y)
+        forward_core(z, at.fx, at.y, None)
+        arrive(recv_sem, z, at.x, at.fy, at.c, None)
+        forward(z, at.x, at.fy, 1, to_x)
+        forward_core(z, at.x, at.fy, None)
+
+    order = [0] + [d for k in range(1, nz) for d in sorted({k, nz - k}) if k <= nz - k]
+    column(order[0])
+    for before, now in zip(order, order[1:]):
+        column(now)
+        turned(before)
+    turned(order[-1])
+    for dz in order:
+        z = at.turn(dz)
+        for h in range(2):
+            arrive(recv_sem, z, at.fx, at.fy, at.c, h)
+            forward_core(z, at.fx, at.fy, h)
+    for dz in order:
+        z = at.turn(dz)
+        arrive(core_sem, z, at.x, at.y, at.fc, None)
+        arrive(core_sem, z, at.fx, at.y, at.fc, None)
+        arrive(core_sem, z, at.x, at.fy, at.fc, None)
+        arrive(core_sem, z, at.fx, at.fy, at.fc, 0)
+        arrive(core_sem, z, at.fx, at.fy, at.fc, 1)
+    for copy in sends:
+        copy.wait_send()
+    local.wait()
+
+
+def gather_rows(own, nz):
+    rows, width = own.shape
+    blocks = nz * 8
+    return pl.pallas_call(
+        functools.partial(gather_kernel, nz),
+        out_shape=jax.ShapeDtypeStruct((blocks, rows, width), own.dtype),
+        in_specs=[pl.BlockSpec(memory_space=pltpu.VMEM)],
+        out_specs=pl.BlockSpec(memory_space=pl.ANY),
+        scratch_shapes=[
+            pltpu.SemaphoreType.DMA((nz * 16,)),
+            pltpu.SemaphoreType.DMA((nz * 8,)),
+            pltpu.SemaphoreType.DMA((nz * 8,)),
+            pltpu.SemaphoreType.DMA,
+        ],
+        compiler_params=pltpu.CompilerParams(collective_id=0, has_side_effects=True),
+        name="gather_rows",
+    )(own)
+
+
+def combine_kernel(
+    nz,
+    combiner_ref,
+    outs_ref,
+    mix_ref,
+    acc,
+    core_in,
+    diag_in,
+    x_in,
+    y_in,
+    z_in,
+    stage,
+    stage_sem,
+    send_sem,
+    recv_sem,
+    core_sem,
+):
+    at = Grid(nz)
+    rows = acc.shape[1]
+    half = rows // 2
+    spots = [(z, x, y) for x, y in ((1, 1), (1, 0), (0, 1), (0, 0)) for z in range(1, nz + 1)]
+    sends = []
+
+    def where(spot):
+        dz, dx, dy = spot
+        return (
+            at.turn(dz % nz),
+            at.fx if dx else at.x,
+            at.fy if dy else at.y,
+        )
+
+    def place(z, x, y):
+        return (z * 2 + x) * 2 + y
+
+    turns = [(spot, c) for spot in spots for c in (at.fc, at.c)]
+
+    def load(i):
+        spot, c = turns[i]
+        return pltpu.make_async_copy(
+            outs_ref.at[block_at(*where(spot), c)], stage.at[i % 3], stage_sem.at[i % 3]
+        )
+
+    load(0).start()
+    load(1).start()
+    at.meet()
+
+    def send(src, dst, sem, to):
+        copy = pltpu.make_async_remote_copy(
+            src_ref=src,
+            dst_ref=dst,
+            send_sem=send_sem.at[len(sends)],
+            recv_sem=sem,
+            device_id=to,
+            device_id_type=MESH,
+        )
+        copy.start()
+        sends.append(copy)
+
+    def arrive(ref, sem):
+        pltpu.make_async_copy(ref, ref, sem).wait()
+
+    def make(i):
+        if i + 2 < len(turns):
+            load(i + 2).start()
+        load(i).wait()
+        spot, c = turns[i]
+        block = block_at(*where(spot), c)
+        slot = i % 3
+
+        @pl.loop(0, acc.shape[2] // 512)
+        def _(k):
+            cols = pl.ds(pl.multiple_of(k * 512, 512), 512)
+            acc[block, :, cols] = jnp.dot(
+                combiner_ref[block], stage[slot, :, cols], preferred_element_type=jnp.float32
+            ).astype(acc.dtype)
+
+        return block
+
+    def add(block, h, others):
+        first, count = (0, rows) if h is None else (h * half, half)
+
+        @pl.loop(0, count // 16)
+        def _(k):
+            at_acc = pl.ds(pl.multiple_of(first + k * 16, 16), 16)
+            total = acc[block, at_acc, :].astype(jnp.float32)
+            for ref, lead in others:
+                total = total + ref[lead, at_acc, :].astype(jnp.float32)
+            acc[block, at_acc, :] = total.astype(acc.dtype)
+
+    to_x = device(at.z, at.fx, at.y, at.c)
+    to_y = device(at.z, at.x, at.fy, at.c)
+    to_core = device(at.z, at.x, at.y, at.fc)
+    for i in range(0, len(turns), 2):
+        spot = turns[i][0]
+        dz, dx, dy = spot
+        z, x, y = where(spot)
+        theirs = make(i)
+        spare = place(z, x, y)
+        send(acc.at[theirs], core_in.at[spare], core_sem.at[spare], to_core)
+        mine = make(i + 1)
+        arrive(core_in.at[spare], core_sem.at[spare])
+        if dx and dy:
+            add(mine, None, [(core_in, spare)])
+            send(
+                acc.at[mine, pl.ds(0, half)],
+                diag_in.at[z, pl.ds(0, half)],
+                recv_sem.at[z],
+                to_y,
+            )
+            send(
+                acc.at[mine, pl.ds(half, half)],
+                diag_in.at[z, pl.ds(half, half)],
+                recv_sem.at[nz + z],
+                to_x,
+            )
+        elif dx:
+            arrive(diag_in.at[z, pl.ds(0, half)], recv_sem.at[z])
+            add(mine, 0, [(core_in, spare), (diag_in, z)])
+            add(mine, 1, [(core_in, spare)])
+            send(acc.at[mine], x_in.at[z], recv_sem.at[2 * nz + z], to_x)
+        elif dy:
+            arrive(diag_in.at[z, pl.ds(half, half)], recv_sem.at[nz + z])
+            add(mine, 0, [(core_in, spare)])
+            add(mine, 1, [(core_in, spare), (diag_in, z)])
+            send(acc.at[mine], y_in.at[z], recv_sem.at[3 * nz + z], to_y)
+        else:
+            arrive(x_in.at[z], recv_sem.at[2 * nz + z])
+            arrive(y_in.at[z], recv_sem.at[3 * nz + z])
+            add(mine, None, [(core_in, spare), (x_in, z), (y_in, z)])
+            if dz % nz:
+                send(
+                    acc.at[mine],
+                    z_in.at[at.z],
+                    recv_sem.at[4 * nz + at.z],
+                    device(z, at.x, at.y, at.c),
+                )
+    others = [at.turn(dz) for dz in range(1, nz)]
+    for z in others:
+        arrive(z_in.at[z], recv_sem.at[4 * nz + z])
+    own = block_at(at.z, at.x, at.y, at.c)
+
+    @pl.loop(0, rows // 16)
+    def _(k):
+        part = pl.ds(pl.multiple_of(k * 16, 16), 16)
+        total = acc[own, part, :].astype(jnp.float32)
+        for z in others:
+            total = total + z_in[z, part, :].astype(jnp.float32)
+        mix_ref[part, :] = total
+
+    for copy in sends:
+        copy.wait_send()
+
+
+def combine_rows(combiner, outs, nz):
+    blocks, rows, slots = combiner.shape
+    width = outs.shape[2]
+    kind = outs.dtype
+    return pl.pallas_call(
+        functools.partial(combine_kernel, nz),
+        out_shape=jax.ShapeDtypeStruct((rows, width), jnp.float32),
+        in_specs=[pl.BlockSpec(memory_space=pltpu.VMEM), pl.BlockSpec(memory_space=pl.ANY)],
+        out_specs=pl.BlockSpec(memory_space=pltpu.VMEM),
+        scratch_shapes=[
+            pltpu.VMEM((blocks, rows, width), kind),
+            pltpu.VMEM((blocks // 2, rows, width), kind),
+            pltpu.VMEM((nz, rows, width), kind),
+            pltpu.VMEM((nz, rows, width), kind),
+            pltpu.VMEM((nz, rows, width), kind),
+            pltpu.VMEM((nz, rows, width), kind),
+            pltpu.VMEM((3, slots, width), kind),
+            pltpu.SemaphoreType.DMA((3,)),
+            pltpu.SemaphoreType.DMA((nz * 10,)),
+            pltpu.SemaphoreType.DMA((nz * 5,)),
+            pltpu.SemaphoreType.DMA((nz * 4,)),
+        ],
+        compiler_params=pltpu.CompilerParams(
+            collective_id=1, has_side_effects=True, vmem_limit_bytes=56 * 1024 * 1024
+        ),
+        name="combine_rows",
+    )(combiner, outs)
 
 
 def entering(array, axis, combine, identity):
@@ -86,22 +418,26 @@
     )
 
 
-def route_tokens(expert_ids, gate_weights, normed, capacity):
-    row_count = expert_ids.shape[0]
-    onehot = (expert_ids[:, :, None] == jnp.arange(E, dtype=jnp.int32)).astype(jnp.int32)
-    flat_hits = onehot.reshape(row_count * TOPK, E)
-    earlier = jnp.cumsum(flat_hits, axis=0) - flat_hits
-    slot_index = jnp.sum(earlier * flat_hits, axis=1).reshape(row_count, TOPK)
-    target = expert_ids * capacity + slot_index
-    placed = (target[:, :, None] == jnp.arange(E * capacity, dtype=jnp.int32)).astype(jnp.float32)
-    dispatch_rows = jnp.sum(placed, axis=1).astype(jnp.bfloat16)
-    combiner = jnp.sum(
-        placed * gate_weights.astype(jnp.bfloat16).astype(jnp.float32)[:, :, None], axis=1
-    ).astype(jnp.bfloat16)
-    buffer = jnp.einsum(
-        "rs,rd->sd", dispatch_rows, normed, preferred_element_type=jnp.float32
-    ).astype(jnp.bfloat16)
-    return (buffer, combiner)
+def local_routes(expert_ids, gate_weights, row_count, local_experts, capacity):
+    blocks = expert_ids.shape[0] // row_count
+    own = lax.axis_index("ctx") * local_experts + jnp.arange(local_experts, dtype=jnp.int32)
+    named = (expert_ids[:, :, None] == own).astype(jnp.float32)
+    gates = jnp.sum(named * gate_weights.astype(jnp.float32)[:, :, None], axis=1)
+    hits = jnp.sum(named, axis=1).reshape(blocks, row_count, local_experts)
+    row = lax.broadcasted_iota(jnp.int32, (row_count, row_count), 0)
+    col = lax.broadcasted_iota(jnp.int32, (row_count, row_count), 1)
+    before = (col < row).astype(jnp.bfloat16)
+    slot = jnp.einsum(
+        "rs,bse->bre", before, hits.astype(jnp.bfloat16), preferred_element_type=jnp.float32
+    )
+    placed = jnp.where(
+        (slot[:, :, :, None] == jnp.arange(capacity, dtype=jnp.float32)) & (hits[:, :, :, None] > 0),
+        1.0,
+        0.0,
+    )
+    combiner = placed * gates.reshape(blocks, row_count, local_experts, 1)
+    flat = (blocks, row_count, local_experts * capacity)
+    return placed.astype(jnp.bfloat16).reshape(flat), combiner.astype(jnp.bfloat16).reshape(flat)
 
 
 def on_device(
@@ -144,12 +480,25 @@
     ).astype(jnp.bfloat16)
     row_count = expert_ids.shape[0]
     capacity = (5 * row_count * TOPK + 4 * E - 1) // (4 * E)
-    buffer, combiner = route_tokens(expert_ids, gate_weights, normed, capacity)
-    ctx_count = lax.axis_size("ctx")
+    capacity = (capacity + 15) // 16 * 16
     local_experts = gate_proj.shape[0]
-    outgoing = buffer.reshape(ctx_count, local_experts, capacity, D)
-    arrived = lax.all_to_all(outgoing, "ctx", split_axis=0, concat_axis=0, tiled=True)
-    block_rows = lax.all_gather(arrived, "grp", axis=0, tiled=True)
+    everyone = ("ctx", "grp")
+    all_ids = lax.all_gather(expert_ids, everyone, axis=0, tiled=True)
+    all_gates = lax.all_gather(gate_weights.astype(jnp.bfloat16), everyone, axis=0, tiled=True)
+    placed, combiner = local_routes(all_ids, all_gates, row_count, local_experts, capacity)
+    blocks = lax.axis_size("ctx") * lax.axis_size("grp")
+    nz = lax.axis_size("ctx") // 2
+    kernels = lax.axis_size("grp") == 4 and blocks * row_count <= VMEM_TOKENS
+    if kernels:
+        all_rows = gather_rows(normed, nz)
+    else:
+        all_rows = lax.all_gather(normed, everyone, axis=0, tiled=True)
+    block_rows = jnp.einsum(
+        "brs,brd->bsd",
+        placed,
+        all_rows.reshape(blocks, row_count, D),
+        preferred_element_type=jnp.float32,
+    ).astype(jnp.bfloat16).reshape(blocks, local_experts, capacity, D)
     gate_part = jnp.einsum(
         "secd,edf->secf", block_rows, gate_proj, preferred_element_type=jnp.float32
     )
@@ -158,11 +507,16 @@
     partial_out = jnp.einsum(
         "secf,efd->secd", hidden, down_proj, preferred_element_type=jnp.float32
     ).astype(jnp.bfloat16)
-    summed = lax.psum_scatter(
-        partial_out.astype(jnp.float32).astype(jnp.bfloat16), "grp", scatter_dimension=0, tiled=True
-    )
-    returned = lax.all_to_all(summed, "ctx", split_axis=0, concat_axis=0, tiled=True)
-    expert_mix = jnp.dot(combiner, returned.reshape(-1, D), preferred_element_type=jnp.float32)
+    partial_rows = partial_out.reshape(blocks, local_experts * capacity, D)
+    if kernels:
+        expert_mix = combine_rows(combiner, partial_rows, nz)
+    else:
+        partial_mix = jnp.einsum(
+            "brs,bsd->brd", combiner, partial_rows, preferred_element_type=jnp.float32
+        ).astype(jnp.bfloat16)
+        expert_mix = lax.psum_scatter(
+            partial_mix.reshape(-1, D), everyone, scatter_dimension=0, tiled=True
+        ).astype(jnp.float32)
     layer_out = (widened + expert_mix).astype(jnp.bfloat16)
     return (attended, layer_out)
 

time: 625 us -> 457 us (0.73); the launches traced: 617 us -> 456 us
  waiting for transfers between devices: 226 us -> 0.02 us
  Pallas kernels: 0 us -> 206 us
  blocking collectives: 223 us -> 116 us
  local copies, waits for them, and re-layouts: 70.4 us -> 28.3 us
    pallas_call x0 -> x2, Pallas kernels: none -> 206 us  [the longest x1 117 us: combine_rows(): pl.pallas_call(functools.partial(combine_kernel, nz), out_shape=jax.Shape...]
    all_to_all x2 -> x0, blocking collectives: 184 us -> none  [the longest x1 92.9 us: on_device(): lax.all_to_all(summed, 'ctx', split_axis=0, concat_axis=0, tiled=True)]
    unnamed x4 -> x1, waiting for transfers between devices: 120 us -> 0.02 us
    all_gather x1 -> x0, waiting for transfers between devices: 97.8 us -> none  [on_device(): block_rows = lax.all_gather(arrived, 'grp', axis=0, tiled=True)]
    all_gather x0 -> x2, blocking collectives: none -> 76.7 us  [the longest x1 38.4 us: on_device(): all_ids = lax.all_gather(expert_ids, everyone, axis=0, tiled=True)]
    unnamed x26 -> x21, local copies, waits for them, and re-layouts: 38.8 us -> 0.98 us
    reshape x6 -> x1, local copies, waits for them, and re-layouts: 15.8 us -> 0.78 us  [the longest x2 9.71 us: on_device(): outgoing = buffer.reshape(ctx_count, local_experts, capacity, D)]
    convert_element_type x0 -> x1, local copies, waits for them, and re-layouts: none -> 14.1 us  [on_device(): partial_out = jnp.einsum('secf,efd->secd', hidden, down_proj, preferred_e...]
  transfers between devices with their start and end apart: 4 -> 2, of which waited for: 3 -> 0; matrix products, arithmetic and copies ran while one was open for 1% -> 4% of each run, Pallas kernels for 0% -> 0%
where the time goes in v1:
time: 457 us; the launch traced here: 456 us
  Pallas kernels  206 us (45%)
  blocking collectives  116 us (25%)
  matrix products  68.3 us (15%)
  local copies, waits for them, and re-layouts  28.3 us (6%)
  other arithmetic  18.7 us (4%)
  between operations  15 us (3%)
    pallas_call x1, Pallas kernels, combine_rows(): pl.pallas_call(functools.partial(combine_kernel, nz), out_shape=jax.Shape...  117 us
    pallas_call x1, Pallas kernels, gather_rows(): pl.pallas_call(functools.partial(gather_kernel, nz), out_shape=jax.ShapeD...  88.9 us
    all_gather x1, blocking collectives, on_device(): all_ids = lax.all_gather(expert_ids, everyone, axis=0, tiled=True)  38.4 us
    all_gather x1, blocking collectives, on_device(): lax.all_gather(gate_weights.astype(jnp.bfloat16), everyone, axis=0, tiled...  38.2 us
    dot_general x1, matrix products, on_device(): jnp.einsum('secf,efd->secd', hidden, down_proj, preferred_element_type=jn...  26.5 us
    unnamed x1, blocking collectives  23.1 us
    all_gather x1, blocking collectives, entering(): lax.all_gather(part.astype(kind), axis)  16.3 us
    dot_general x1, matrix products, on_device(): jnp.einsum('secd,edf->secf', block_rows, up_proj, preferred_element_type=...  15.7 us
  transfers between devices with their start and end apart: 2, of which 0 were waited for; matrix products, arithmetic and copies ran while one was open for 4% of the time, Pallas kernels for 0%

profile of v1, /device:TPU:0, one launch (start us, length us, event | category | flops | bytes accessed | tf_op | source)
XLA Modules:
  0.0 456.5 jit_solution(132734930695462096)
XLA Ops:
  7.3 0.8 reshape.155
  8.1 1.2 reduce-window.6
  9.4 0.2 reduce-window.9
  10.1 0.3 copy.125
  10.4 1.6 multiply_reduce_fusion
  12.0 0.2 copy.127
  12.2 1.0 convolution_convert_fusion.1
  13.2 0.6 dynamic-slice
  14.5 0.2 dynamic-update-slice
  14.7 23.1 %all-reduce = bf16[32]{0:T(256)(128)(2,1)S(1)} all-reduce(bf16[32]{0:T(256)(128)(2,1)S(1)} %dynamic-update-slice), channel_id=2, replica_groups=mesh['ctx'=8,'grp'=4] {'ctx'}, use_global_device_ids=true, to_apply=%add | all-reduce | flops 32 | bytes 128
  38.0 38.2 %all_gather.25 = bf16[4096,6]{0,1:T(8,128)(2,1)S(1)} all-gather(bf16[128,6]{0,1:T(8,128)(2,1)S(1)} %convert_element_type.169), channel_id=1, replica_groups=mesh['ctx'=8,'grp'=4] {'ctx','grp'}, dimensions={0}, use_global_device_ids=true | all-gather | bytes 50688 | tf_op jit(solution)/shard_map/all_gather | solution.py:487
  76.2 16.3 %all_gather.23 = bf16[8,4,128]{2,1,0:T(4,128)(2,1)S(1)} all-gather(bf16[1,4,128]{2,1,0:T(4,128)(2,1)S(1)} %bitcast.171), channel_id=1, replica_groups=mesh['ctx'=8,'grp'=4] {'ctx'}, dimensions={0}, use_global_device_ids=true | all-gather | bytes 9216 | tf_op jit(solution)/shard_map/all_gather | solution.py:347
  92.5 38.4 %all_gather.24 = s32[4096,6]{0,1:T(8,128)S(1)} all-gather(s32[128,6]{0,1:T(8,128)S(1)} %copy-done.4), channel_id=1, replica_groups=mesh['ctx'=8,'grp'=4] {'ctx','grp'}, dimensions={0}, use_global_device_ids=true | all-gather | bytes 101376 | tf_op jit(solution)/shard_map/all_gather | solution.py:486
  131.0 0.2 fusion.52
  131.2 0.2 convolution_bitcast_fusion.1
  131.4 1.9 fusion.18
  133.3 2.7 fusion.33
  136.0 9.0 %while.16 = (s32[]{:T(128)}, f32[4,128,128]{2,1,0:T(8,128)S(1)}, f32[4,128]{1,0:T(4,128)S(1)}, s32[]{:T(128)}, bf16[8,4]{1,0:T(8,128)(2,1)S(1)}, /*index=5*/bf16...) while((s32[]{:T(128)}, f32[4,128,128]{2,1,0:T(8,128)S(1)}, ...), condition=%wide.region_4.5_spmd.clone, body=%wide.region_3.4_spmd.clone.sunk | while | flops 330248 | bytes 660671 | solution.py:364
  136.1 1.0 fusion.96
  137.2 1.0 fusion.96
  138.4 1.0 fusion.96
  139.5 1.0 fusion.96
  140.6 1.0 fusion.96
  141.8 1.0 fusion.96
  142.9 1.0 fusion.96
  144.0 1.0 fusion.96
  145.1 1.4 fusion.51
  146.5 2.7 fusion.38
  149.2 0.4 copy.107
  149.6 1.0 all_to_all.14
  150.6 4.3 all-to-all-start
  155.0 0.2 and.13
  155.2 0.6 copy.110
  155.8 1.5 eq.37
  157.3 1.9 copy.109
  159.3 1.5 mul.129
  160.7 2.9 copy.111
  163.7 3.3 fusion.29
  167.0 1.3 copy.108
  168.3 4.8 %fusion.39 = (f32[128]{0:T(128)S(1)}, bf16[128,2048]{1,0:T(8,128)(2,1)S(1)}) fusion(bf16[128,2048]{0,1:T(8,128)(2,1)S(1)} %bitcast.160, bf16[2048,2048]{1,0:T(8,128)(2,1)} %param.19, bf16[128,2048]{1,0:T(8,128)(2,1)} %param.18), kind=kOutput, calls=%fused_computation.50 | convolution fusion | flops 1075314560 | bytes 9961984 | tf_op jit(solution)/shard_map/dot_general | solution.py:475
  173.1 1.0 fusion.41.own_ref
  174.1 88.9 %gather_rows.1 = bf16[32,128,2048]{2,1,0:T(8,128)(2,1)} custom-call(bf16[128,2048]{1,0:T(8,128)(2,1)} %fusion.41.own_ref), custom_call_target="tpu_custom_call" | custom-call | tf_op jit(solution)/shard_map/gather_rows/pallas_call | solution.py:146
  263.0 11.5 %convolution_convert_fusion = bf16[32,128,2048]{2,1,0:T(8,128)(2,1)} fusion(bf16[32,128,2048]{2,1,0:T(8,128)(2,1)} %gather_rows.1, pred[32,128,128]{2,1,0:T(32,128)(4,1)S(1)} %get-tuple-element.170), kind=kOutput, calls=%fused_computation.13 | convolution fusion | flops 2156920832 | bytes 34078720 | tf_op jit(solution)/shard_map/brs,brd->bsd/dot_general | solution.py:496
  274.5 15.7 %fusion.5 = f32[8,32,16,352]{3,2,1,0:T(8,128)} fusion(bf16[32,8,16,2048]{3,2,1,0:T(8,128)(2,1)} %bitcast.155, bf16[8,2048,352]{1,2,0:T(8,128)(2,1)} %param.24), kind=kOutput, calls=%fused_computation.9 | convolution fusion | flops 5905580032 | bytes 34078720 | tf_op jit(solution)/shard_map/secd,edf->secf/dot_general | solution.py:505
  290.2 26.5 %convert_bitcast_fusion = bf16[32,8,16,2048]{3,2,0,1:T(8,128)(2,1)} fusion(bf16[8,352,2048]{2,1,0:T(8,128)(2,1)} %param.25, f32[8,32,16,352]{3,2,1,0:T(8,128)} %fusion.5, bf16[32,8,16,2048]{3,2,1,0:T(8,128)(2,1)} %bitcast.156, bf16[8,2048,352]{1,2,0:T(8,128)(2,1)} %param.23), kind=kOutput, calls=%fused_computation.8 | convolution fusion | flops 11828199424 | bytes 62390272 | tf_op jit(solution)/shard_map/secf,efd->secd/dot_general | solution.py:507
  316.7 14.1 %copy.115 = bf16[32,8,16,2048]{3,2,1,0:T(8,128)(2,1)} copy(bf16[32,8,16,2048]{3,2,0,1:T(8,128)(2,1)} %convert_bitcast_fusion) | data formatting | bytes 33554432 | tf_op jit(solution)/shard_map/convert_element_type | solution.py:509
  330.8 116.7 %combine_rows.1 = f32[128,2048]{1,0:T(8,128)} custom-call(bf16[32,128,128]{2,1,0:T(8,128)(2,1)} %get-tuple-element.169.combiner_ref, bf16[32,128,2048]{2,1,0:T(8,128)(2,1)} %bitcast.154), custom_call_target="tpu_custom_call" | custom-call | tf_op jit(solution)/shard_map/combine_rows/pallas_call | solution.py:319
  447.5 2.1 fusion.42
  (57 shorter events, 1.8 us)
Async XLA Ops:
  7.2 5.1 %copy-start = (bf16[512,512]{1,0:T(8,128)(2,1)S(1)}, bf16[512,512]{1,0:T(8,128)(2,1)}, u32[]{:S(2)}) copy-start(bf16[512,512]{1,0:T(8,128)(2,1)} %param.16) | copy-start | bytes 1572868
  7.2 6.0 %copy-start.7 = (u32[32]{0:T(128)S(1)}, u32[32]{0:T(128)}, u32[]{:S(2)}) copy-start(u32[32]{0:T(128)} %constant.59) | copy-start | bytes 388
  7.2 30.7 %copy-start.5 = (f32[128,6]{0,1:T(8,128)S(1)}, f32[128,6]{0,1:T(8,128)}, u32[]{:S(2)}) copy-start(f32[128,6]{0,1:T(8,128)} %param.22) | copy-start | bytes 9220
  7.2 85.3 %copy-start.4 = (s32[128,6]{0,1:T(8,128)S(1)}, s32[128,6]{0,1:T(8,128)}, u32[]{:S(2)}) copy-start(s32[128,6]{0,1:T(8,128)} %param.21) | copy-start | bytes 9220
  7.2 124.2 %copy-start.6 = (bf16[512,512]{1,0:T(8,128)(2,1)S(1)}, bf16[512,512]{1,0:T(8,128)(2,1)}, u32[]{:S(2)}) copy-start(bf16[512,512]{1,0:T(8,128)(2,1)} %param.14) | copy-start | bytes 1572868
  7.2 128.8 %all-gather.4.cloned.1.call-start = ((), (), s32[]{:S(2)}) async-start(), calls=%async_computation.1 | async-start | bytes 1179648 | tf_op jit(solution)/shard_map/all_gather | solution.py:347
  150.6 16.4 %all-to-all-start = ((bf16[4,128,512]{2,1,0:T(8,128)(2,1)}), bf16[4,128,512]{2,1,0:T(8,128)(2,1)}, u32[]{:S(2)}, u32[]{:S(2)}) async-start(bf16[4,128,512]{2,1,0:T(8,128)(2,1)} %all_to_all.14), calls=%async_computation | async-start | bytes 1048576 | tf_op jit(solution)/shard_map/all_to_all | solution.py:474
  168.3 4.9 %copy-start.3 = (f32[2048]{0:T(1024)S(1)}, f32[2048]{0:T(1024)}, u32[]{:S(2)}) copy-start(f32[2048]{0:T(1024)} %param.20) | copy-start | bytes 24580
  173.1 274.4 %copy-start.2 = (bf16[128,2048]{1,0:T(8,128)(2,1)}, bf16[128,2048]{1,0:T(8,128)(2,1)S(1)}, u32[]{:S(2)}) copy-start(bf16[128,2048]{1,0:T(8,128)(2,1)S(1)} %get-tuple-element.178) | copy-start | bytes 1572868
  330.8 118.8 %copy-start.1 = (bf16[512,512]{1,0:T(8,128)(2,1)S(1)}, bf16[512,512]{1,0:T(8,128)(2,1)}, u32[]{:S(2)}) copy-start(bf16[512,512]{1,0:T(8,128)(2,1)} %param.16) | copy-start | bytes 1572868
Sparse Core Ops, SparseCore 0:
  13.3 43.0 all-gather.3

commit v2 on v1

--- a/solution.py
+++ b/solution.py
@@ -193,7 +193,12 @@
     def place(z, x, y):
         return (z * 2 + x) * 2 + y
 
-    turns = [(spot, c) for spot in spots for c in (at.fc, at.c)]
+    ahead = 3
+    turns = [(spot, at.fc) for spot in spots[:ahead]]
+    for i, spot in enumerate(spots):
+        turns.append((spot, at.c))
+        if i + ahead < len(spots):
+            turns.append((spots[i + ahead], at.fc))
 
     def load(i):
         spot, c = turns[i]
@@ -251,14 +256,25 @@
     to_x = device(at.z, at.fx, at.y, at.c)
     to_y = device(at.z, at.x, at.fy, at.c)
     to_core = device(at.z, at.x, at.y, at.fc)
-    for i in range(0, len(turns), 2):
-        spot = turns[i][0]
+    made = 0
+
+    def give(i):
+        spare = place(*where(spots[i]))
+        theirs = make(made)
+        send(acc.at[theirs], core_in.at[spare], core_sem.at[spare], to_core)
+
+    for i in range(ahead):
+        give(i)
+        made += 1
+    for i, spot in enumerate(spots):
         dz, dx, dy = spot
         z, x, y = where(spot)
-        theirs = make(i)
         spare = place(z, x, y)
-        send(acc.at[theirs], core_in.at[spare], core_sem.at[spare], to_core)
-        mine = make(i + 1)
+        mine = make(made)
+        made += 1
+        if i + ahead < len(spots):
+            give(i + ahead)
+            made += 1
         arrive(core_in.at[spare], core_sem.at[spare])
         if dx and dy:
             add(mine, None, [(core_in, spare)])
@@ -341,27 +357,193 @@
     )(combiner, outs)
 
 
-def entering(array, axis, combine, identity):
-    count, index = (lax.axis_size(axis), lax.axis_index(axis))
-    everything = jax.tree.map(
-        lambda part, kind: lax.all_gather(part.astype(kind), axis),
-        array,
-        (jnp.bfloat16, jnp.bfloat16, jnp.bfloat16),
-    )
-    start = jax.tree.map(
-        lambda part, zero: jnp.broadcast_to(jnp.asarray(zero, part.dtype), part.shape),
-        array,
-        identity,
-    )
-
-    def lap(k, before):
-        reached = k < index
-        new = combine(
-            before, jax.tree.map(lambda part, own: part[k].astype(own.dtype), everything, array)
-        )
-        return jax.tree.map(lambda a, b: jnp.where(reached, a, b), new, before)
-
-    return lax.fori_loop(0, count, lap, start)
+def share_kernel(
+    nz, route_ref, state_ref, routes_ref, states_ref, send_sem, z_sem, x_sem, small_sem, far_sem
+):
+    at = Grid(nz)
+    routes_ref[at.z, at.x, at.y, at.c] = route_ref[...]
+    states_ref[at.z, at.x] = state_ref[...]
+    at.meet()
+    sends = []
+
+    def send(ref, sem, to):
+        copy = pltpu.make_async_remote_copy(
+            src_ref=ref,
+            dst_ref=ref,
+            send_sem=send_sem.at[len(sends)],
+            recv_sem=sem,
+            device_id=to,
+            device_id_type=MESH,
+        )
+        copy.start()
+        sends.append(copy)
+
+    def arrive(ref, sem):
+        pltpu.make_async_copy(ref, ref, sem).wait()
+
+    to_x = device(at.z, at.fx, at.y, at.c)
+    to_y = device(at.z, at.x, at.fy, at.c)
+    to_core = device(at.z, at.x, at.y, at.fc)
+    send(routes_ref.at[at.z, at.x, at.y, at.c], small_sem.at[0], to_x)
+    send(states_ref.at[at.z, at.x], x_sem.at[at.z], to_x)
+    for dz in range(1, nz):
+        send(
+            states_ref.at[at.z, at.x], z_sem.at[at.z], device(at.turn(dz), at.x, at.y, at.c)
+        )
+    arrive(routes_ref.at[at.z, at.fx, at.y, at.c], small_sem.at[0])
+    send(routes_ref.at[at.z, :, at.y, at.c], small_sem.at[1], to_y)
+    arrive(routes_ref.at[at.z, :, at.fy, at.c], small_sem.at[1])
+    send(routes_ref.at[at.z, :, :, at.c], small_sem.at[2], to_core)
+    arrive(routes_ref.at[at.z, :, :, at.fc], small_sem.at[2])
+    for dz in range(1, nz):
+        send(routes_ref.at[at.z], far_sem.at[at.z], device(at.turn(dz), at.x, at.y, at.c))
+    for dz in range(1, nz):
+        z = at.turn(dz)
+        arrive(states_ref.at[z, at.x], z_sem.at[z])
+        send(states_ref.at[z, at.x], x_sem.at[z], to_x)
+    for dz in range(nz):
+        z = at.turn(dz)
+        arrive(states_ref.at[z, at.fx], x_sem.at[z])
+        if dz:
+            arrive(routes_ref.at[z], far_sem.at[z])
+    for copy in sends:
+        copy.wait_send()
+
+
+def share(route, state, nz):
+    routes, states = pl.pallas_call(
+        functools.partial(share_kernel, nz),
+        out_shape=(
+            jax.ShapeDtypeStruct((nz, 2, 2, 2) + route.shape, route.dtype),
+            jax.ShapeDtypeStruct((nz, 2) + state.shape, state.dtype),
+        ),
+        in_specs=[pl.BlockSpec(memory_space=pltpu.VMEM)] * 2,
+        out_specs=(pl.BlockSpec(memory_space=pltpu.VMEM),) * 2,
+        scratch_shapes=[
+            pltpu.SemaphoreType.DMA((3 * nz + 4,)),
+            pltpu.SemaphoreType.DMA((nz,)),
+            pltpu.SemaphoreType.DMA((nz,)),
+            pltpu.SemaphoreType.DMA((3,)),
+            pltpu.SemaphoreType.DMA((nz,)),
+        ],
+        compiler_params=pltpu.CompilerParams(collective_id=2, has_side_effects=True),
+        name="share",
+    )(route, state)
+    return routes.reshape((nz * 8,) + route.shape), states.reshape((nz * 2,) + state.shape)
+
+
+def expert_kernel(
+    waves, slots, first_ref, rows_ref, routes_ref, gate_ref, up_ref, down_ref, out_ref, mix_ref, x_ref
+):
+    step = pl.program_id(0)
+    experts = x_ref.shape[0]
+    count, rows = rows_ref.shape[0], rows_ref.shape[1]
+
+    @pl.when(step < waves)
+    def _():
+        row = lax.broadcasted_iota(jnp.int32, (rows, rows), 0)
+        col = lax.broadcasted_iota(jnp.int32, (rows, rows), 1)
+        before = (row < col).astype(jnp.bfloat16)
+        own = (
+            lax.broadcasted_iota(jnp.int32, (experts, rows), 0) + first_ref[0] * experts
+        ).astype(jnp.float32)
+        spot = lax.broadcasted_iota(jnp.int32, (experts, slots, rows), 1).astype(jnp.float32)
+        for b in range(count):
+            info = routes_ref[b].astype(jnp.float32)
+            hits = jnp.zeros((experts, rows), jnp.float32)
+            gates = jnp.zeros((experts, rows), jnp.float32)
+            for k in range(TOPK):
+                same = info[k : k + 1, :] == own
+                hits = jnp.where(same, 1.0, hits)
+                gates = jnp.where(same, info[TOPK + k : TOPK + k + 1, :], gates)
+            slot = jnp.dot(hits.astype(jnp.bfloat16), before, preferred_element_type=jnp.float32)
+            slot = jnp.where(hits > 0, slot, -1.0)
+            placed = jnp.where(slot[:, None, :] == spot, 1.0, 0.0)
+            weighed = (placed * gates[:, None, :]).reshape(experts * slots, rows)
+            mix_ref[b] = weighed.T.astype(jnp.bfloat16)
+            placed = placed.reshape(experts * slots, rows).astype(jnp.bfloat16)
+            picked = jnp.dot(placed, rows_ref[b], preferred_element_type=jnp.float32)
+            picked = picked.astype(jnp.bfloat16)
+            start = pl.multiple_of((step * count + b) * slots, slots)
+            for e in range(experts):
+                x_ref[e, pl.ds(start, slots), :] = picked[e * slots : (e + 1) * slots]
+
+    @pl.when(step >= waves)
+    def _():
+        e = step - waves
+        total = x_ref.shape[1]
+        part = min(total, 256)
+        for p in range(0, total, part):
+            x = x_ref[e, p : p + part, :]
+            gate = jnp.dot(x, gate_ref[0], preferred_element_type=jnp.float32)
+            up = jnp.dot(x, up_ref[0], preferred_element_type=jnp.float32)
+            hidden = (jax.nn.silu(gate) * up).astype(jnp.bfloat16)
+            made = jnp.dot(hidden, down_ref[0], preferred_element_type=jnp.float32)
+            out_ref[p // slots : (p + part) // slots, 0] = made.astype(jnp.bfloat16).reshape(
+                part // slots, slots, made.shape[1]
+            )
+
+
+def run_experts(all_rows, routes, gate_proj, up_proj, down_proj, slots):
+    blocks, rows, width = all_rows.shape
+    experts, _, units = gate_proj.shape
+    count = 4
+    waves = blocks // count
+    first = lax.axis_index("ctx").astype(jnp.int32).reshape(1)
+    wave = lambda i: (jnp.minimum(i, waves - 1), 0, 0)
+    turn = lambda i: (jnp.maximum(i - waves, 0), 0, 0)
+    out, mix = pl.pallas_call(
+        functools.partial(expert_kernel, waves, slots),
+        grid=(waves + experts,),
+        out_shape=(
+            jax.ShapeDtypeStruct((blocks, experts, slots, width), jnp.bfloat16),
+            jax.ShapeDtypeStruct((blocks, rows, experts * slots), jnp.bfloat16),
+        ),
+        in_specs=[
+            pl.BlockSpec(memory_space=pltpu.SMEM),
+            pl.BlockSpec((count, rows, width), wave),
+            pl.BlockSpec((count,) + routes.shape[1:], wave),
+            pl.BlockSpec((1, width, units), turn),
+            pl.BlockSpec((1, width, units), turn),
+            pl.BlockSpec((1, units, width), turn),
+        ],
+        out_specs=(
+            pl.BlockSpec((blocks, 1, slots, width), lambda i: (0, jnp.maximum(i - waves, 0), 0, 0)),
+            pl.BlockSpec((count, rows, experts * slots), wave),
+        ),
+        scratch_shapes=[pltpu.VMEM((experts, blocks * slots, width), jnp.bfloat16)],
+        compiler_params=pltpu.CompilerParams(
+            dimension_semantics=("arbitrary",), vmem_limit_bytes=56 * 1024 * 1024
+        ),
+        name="run_experts",
+    )(first, all_rows, routes, gate_proj, up_proj, down_proj)
+    return out.reshape(blocks, experts * slots, width), mix
+
+
+def pack_route(expert_ids, gate_weights):
+    info = jnp.concatenate([expert_ids.astype(jnp.bfloat16), gate_weights.astype(jnp.bfloat16)], 1)
+    return jnp.pad(info.T, ((0, 16 - 2 * TOPK), (0, 0)))
+
+
+def pack_state(total, state, norm):
+    high = total.astype(jnp.bfloat16)
+    low = (total - high.astype(jnp.float32)).astype(jnp.bfloat16)
+    wide = lambda one: jnp.broadcast_to(one[:, None, None], (one.shape[0], 1, HD))
+    packed = jnp.concatenate(
+        [state.astype(jnp.bfloat16), norm.astype(jnp.bfloat16)[:, None], wide(high), wide(low)], 1
+    )
+    return jnp.pad(packed, ((0, 0), (0, 13), (0, 0)))
+
+
+def prior_of(packs):
+    count, index = packs.shape[0], lax.axis_index("ctx")
+    totals = packs[:, :, HD + 1, 0].astype(jnp.float32) + packs[:, :, HD + 2, 0].astype(jnp.float32)
+    of = jnp.arange(count)
+    between = (of[None, :] > of[:, None]) & (of[None, :] < index)
+    spans = jnp.sum(jnp.where(between[:, :, None], totals[None], 0.0), axis=1)
+    factor = jnp.where((of < index)[:, None], jnp.exp(spans), 0.0)
+    prior = jnp.sum(factor[:, :, None, None] * packs[:, :, : HD + 1].astype(jnp.float32), axis=0)
+    return prior[:, :HD], prior[:, HD]
 
 
 def feature_map(values):
@@ -405,17 +587,6 @@
         jnp.bfloat16
     )
     return mixed_rows.reshape(length, -1)
-
-
-def merge_states(earlier_part, later_part):
-    first_total, first_state, first_norm = earlier_part
-    second_total, second_state, second_norm = later_part
-    factor = jnp.exp(second_total)
-    return (
-        first_total + second_total,
-        factor[:, None, None] * first_state + second_state,
-        factor[:, None] * first_norm + second_norm,
-    )
 
 
 def local_routes(expert_ids, gate_weights, row_count, local_experts, capacity):
@@ -460,14 +631,17 @@
     feat_key = feature_map(key_heads).reshape(length, local_heads, HD)
     value_rows = value_heads.reshape(length, local_heads, HD)
     cumulative, block_total, shard_state, local_norm = summarize(feat_key, value_rows, log_decay)
-    start_state = (
-        jnp.zeros_like(block_total),
-        jnp.zeros_like(shard_state),
-        jnp.zeros_like(local_norm),
-    )
-    _, preceding_state, prior_norm = entering(
-        (block_total, shard_state, local_norm), "ctx", merge_states, start_state
-    )
+    row_count = expert_ids.shape[0]
+    blocks = lax.axis_size("ctx") * lax.axis_size("grp")
+    nz = lax.axis_size("ctx") // 2
+    everyone = ("ctx", "grp")
+    kernels = lax.axis_size("grp") == 4 and nz > 1 and blocks * row_count <= VMEM_TOKENS
+    packed = pack_state(block_total, shard_state, local_norm)
+    if kernels:
+        routes, packs = share(pack_route(expert_ids, gate_weights), packed, nz)
+    else:
+        packs = lax.all_gather(packed, "ctx")
+    preceding_state, prior_norm = prior_of(packs)
     mixed_rows = block_output(
         feat_query, feat_key, value_rows, cumulative, preceding_state, prior_norm
     )
@@ -478,41 +652,41 @@
     normed = (
         widened * lax.rsqrt(jnp.mean(widened * widened, axis=1, keepdims=True) + 1e-06) * norm_gain
     ).astype(jnp.bfloat16)
-    row_count = expert_ids.shape[0]
+    local_experts = gate_proj.shape[0]
     capacity = (5 * row_count * TOPK + 4 * E - 1) // (4 * E)
     capacity = (capacity + 15) // 16 * 16
-    local_experts = gate_proj.shape[0]
-    everyone = ("ctx", "grp")
-    all_ids = lax.all_gather(expert_ids, everyone, axis=0, tiled=True)
-    all_gates = lax.all_gather(gate_weights.astype(jnp.bfloat16), everyone, axis=0, tiled=True)
-    placed, combiner = local_routes(all_ids, all_gates, row_count, local_experts, capacity)
-    blocks = lax.axis_size("ctx") * lax.axis_size("grp")
-    nz = lax.axis_size("ctx") // 2
-    kernels = lax.axis_size("grp") == 4 and blocks * row_count <= VMEM_TOKENS
     if kernels:
         all_rows = gather_rows(normed, nz)
-    else:
-        all_rows = lax.all_gather(normed, everyone, axis=0, tiled=True)
-    block_rows = jnp.einsum(
-        "brs,brd->bsd",
-        placed,
-        all_rows.reshape(blocks, row_count, D),
-        preferred_element_type=jnp.float32,
-    ).astype(jnp.bfloat16).reshape(blocks, local_experts, capacity, D)
-    gate_part = jnp.einsum(
-        "secd,edf->secf", block_rows, gate_proj, preferred_element_type=jnp.float32
-    )
-    up_part = jnp.einsum("secd,edf->secf", block_rows, up_proj, preferred_element_type=jnp.float32)
-    hidden = (jax.nn.silu(gate_part) * up_part).astype(jnp.bfloat16)
-    partial_out = jnp.einsum(
-        "secf,efd->secd", hidden, down_proj, preferred_element_type=jnp.float32
-    ).astype(jnp.bfloat16)
-    partial_rows = partial_out.reshape(blocks, local_experts * capacity, D)
-    if kernels:
+        partial_rows, combiner = run_experts(
+            all_rows, routes, gate_proj, up_proj, down_proj, capacity
+        )
         expert_mix = combine_rows(combiner, partial_rows, nz)
     else:
+        all_ids = lax.all_gather(expert_ids, everyone, axis=0, tiled=True)
+        all_gates = lax.all_gather(gate_weights.astype(jnp.bfloat16), everyone, axis=0, tiled=True)
+        placed, combiner = local_routes(all_ids, all_gates, row_count, local_experts, capacity)
+        all_rows = lax.all_gather(normed, everyone, axis=0, tiled=True)
+        block_rows = jnp.einsum(
+            "brs,brd->bsd",
+            placed,
+            all_rows.reshape(blocks, row_count, D),
+            preferred_element_type=jnp.float32,
+        ).astype(jnp.bfloat16).reshape(blocks, local_experts, capacity, D)
+        gate_part = jnp.einsum(
+            "secd,edf->secf", block_rows, gate_proj, preferred_element_type=jnp.float32
+        )
+        up_part = jnp.einsum(
+            "secd,edf->secf", block_rows, up_proj, preferred_element_type=jnp.float32
+        )
+        hidden = (jax.nn.silu(gate_part) * up_part).astype(jnp.bfloat16)
+        partial_out = jnp.einsum(
+            "secf,efd->secd", hidden, down_proj, preferred_element_type=jnp.float32
+        ).astype(jnp.bfloat16)
         partial_mix = jnp.einsum(
-            "brs,bsd->brd", combiner, partial_rows, preferred_element_type=jnp.float32
+            "brs,bsd->brd",
+            combiner,
+            partial_out.reshape(blocks, local_experts * capacity, D),
+            preferred_element_type=jnp.float32,
         ).astype(jnp.bfloat16)
         expert_mix = lax.psum_scatter(
             partial_mix.reshape(-1, D), everyone, scatter_dimension=0, tiled=True

time: 457 us -> 347 us (0.76)
  blocking collectives: 116 us -> 0 us
  Pallas kernels: 206 us -> 282 us
  matrix products: 68.3 us -> 11.7 us
  between operations: 15 us -> 0.86 us
  other arithmetic: 18.7 us -> 10.2 us
  local copies, waits for them, and re-layouts: 28.3 us -> 36.6 us
    all_gather x3 -> x0, blocking collectives: 92.9 us -> none  [the longest x1 38.4 us: on_device(): all_ids = lax.all_gather(expert_ids, everyone, axis=0, tiled=True)]
    pallas_call x0 -> x2, Pallas kernels: none -> 73.7 us  [the longest x1 45.3 us: run_experts(): pl.pallas_call(functools.partial(expert_kernel, waves, slots), grid=(wave...]
    dot_general x4 -> x0, matrix products: 53.9 us -> none  [the longest x1 26.5 us: on_device(): jnp.einsum('secf,efd->secd', hidden, down_proj, preferred_element_type=jn...]
    unnamed x21 -> x18, local copies, waits for them, and re-layouts: 0.98 us -> 31.5 us
    unnamed x1 -> x0, blocking collectives: 23.1 us -> none
    convert_element_type x1, local copies, waits for them, and re-layouts: 14.1 us -> 0.01 us  [pack_state(): norm.astype(jnp.bfloat16)[:, None]]
    select_n x16 -> x1, other arithmetic: 8.74 us -> 0.01 us  [prior_of(): factor = jnp.where((of < index)[:, None], jnp.exp(spans), 0.0)]
    pallas_call x1, Pallas kernels: 88.9 us -> 93.9 us  [gather_rows(): pl.pallas_call(functools.partial(gather_kernel, nz), out_shape=jax.ShapeD...]
  transfers between devices with their start and end apart: 2 -> 1, of which waited for: 0 -> 0; matrix products, arithmetic and copies ran while one was open for 4% -> 9% of each run, Pallas kernels for 0% -> 0%
where the time goes in v2:
time: 347 us; the launch traced here: 345 us
  Pallas kernels  282 us (81%)
  local copies, waits for them, and re-layouts  36.6 us (11%)
  matrix products  11.7 us (3%)
  other arithmetic  10.2 us (3%)
  starting transfers between devices  3.65 us (1%)
    pallas_call x1, Pallas kernels, combine_rows(): pl.pallas_call(functools.partial(combine_kernel, nz), out_shape=jax.Shape...  115 us
    pallas_call x1, Pallas kernels, gather_rows(): pl.pallas_call(functools.partial(gather_kernel, nz), out_shape=jax.ShapeD...  93.9 us
    pallas_call x1, Pallas kernels, run_experts(): pl.pallas_call(functools.partial(expert_kernel, waves, slots), grid=(wave...  45.3 us
    unnamed x18, local copies, waits for them, and re-layouts  31.5 us
    pallas_call x1, Pallas kernels, share(): pl.pallas_call(functools.partial(share_kernel, nz), out_shape=(jax.ShapeD...  28.4 us
  transfers between devices with their start and end apart: 1, of which 0 were waited for; matrix products, arithmetic and copies ran while one was open for 9% of the time, Pallas kernels for 0%

profile of v2, /device:TPU:0, one launch (start us, length us, event | category | flops | bytes accessed | tf_op | source)
XLA Modules:
  0.0 345.3 jit_solution(13124791249169141619)
XLA Ops:
  0.6 0.0 copy-start
  0.7 0.8 reshape.183
  1.4 1.2 reduce-window.6
  2.6 0.2 slice_reduce_fusion
  2.8 0.2 reduce-window.9
  3.0 0.1 add_bitcast_fusion
  3.0 0.1 slice.33
  3.1 0.1 copy.90
  3.2 0.1 iota_compare_fusion
  3.3 0.7 convert_element_type.120
  4.0 0.7 convert_element_type.121
  4.7 0.1 exponential_bitcast_fusion.1
  4.8 0.1 mul.52
  4.9 0.0 copy-start.5
  4.9 0.3 copy.89
  5.3 1.6 multiply_reduce_fusion.1
  6.9 0.2 copy.94
  7.1 0.6 pad.8.route_ref
  7.7 0.3 convolution_convert_fusion
  8.0 0.1 broadcast_in_dim.87
  8.1 0.1 broadcast_in_dim.86
  8.2 0.7 fusion.45.state_ref
  8.9 28.4 %share.1 = (bf16[4,2,2,2,16,128]{5,4,3,2,1,0:T(8,128)(2,1)}, bf16[4,2,4,144,128]{4,3,2,1,0:T(8,128)(2,1)}) custom-call(bf16[16,128]{1,0:T(8,128)(2,1)} %pad.8.route_ref, bf16[4,144,128]{2,1,0:T(8,128)(2,1)} %fusion.45.state_ref), custom_call_target="tpu_custom_call" | custom-call | tf_op jit(solution)/shard_map/share/pallas_call | solution.py:414
  37.3 1.0 fusion.49
  38.2 0.1 copy.91
  38.3 0.1 copy.92
  38.4 0.1 select_reduce_fusion
  38.5 0.1 copy.77
  38.6 1.6 multiply_reduce_fusion
  40.2 1.9 fusion
  42.2 1.7 fusion.6
  43.9 1.4 fusion.22
  45.3 1.7 fusion.11
  47.0 0.4 copy.81
  47.4 1.0 all_to_all.14
  48.4 3.7 %all-to-all-start = ((bf16[4,128,512]{2,1,0:T(8,128)(2,1)}), bf16[4,128,512]{2,1,0:T(8,128)(2,1)S(1)}, u32[]{:S(2)}, u32[]{:S(2)}) async-start(bf16[4,128,512]{2,1,0:T(8,128)(2,1)} %all_to_all.14), calls=%async_computation | async-start | bytes 1048576 | tf_op jit(solution)/shard_map/all_to_all | solution.py:648
  52.0 15.6 %copy.83.gate_ref = bf16[8,2048,352]{2,1,0:T(8,128)(2,1)} copy(bf16[8,2048,352]{1,2,0:T(8,128)(2,1)} %param.21) | data formatting | bytes 23068672 | tf_op args[9]
  67.7 15.5 %copy.84.up_ref = bf16[8,2048,352]{2,1,0:T(8,128)(2,1)} copy(bf16[8,2048,352]{1,2,0:T(8,128)(2,1)} %param.22) | data formatting | bytes 23068672 | tf_op args[10]
  83.2 0.0 all-to-all-done
  83.2 0.3 copy.82
  83.5 0.0 copy-start.4
  83.5 4.8 %fusion.12 = (f32[128]{0:T(128)S(1)}, bf16[128,2048]{1,0:T(8,128)(2,1)S(1)}) fusion(bf16[128,2048]{0,1:T(8,128)(2,1)S(1)} %bitcast.94, bf16[2048,2048]{1,0:T(8,128)(2,1)} %param.17, bf16[128,2048]{1,0:T(8,128)(2,1)S(1)} %copy-done.3), kind=kOutput, calls=%fused_computation.21 | convolution fusion | flops 1075314560 | bytes 9961984 | tf_op jit(solution)/shard_map/dot_general | solution.py:649
  88.2 0.0 copy-start.2
  88.3 1.0 fusion.14.own_ref
  89.3 93.9 %gather_rows.1.rows_ref = bf16[32,128,2048]{2,1,0:T(8,128)(2,1)} custom-call(bf16[128,2048]{1,0:T(8,128)(2,1)} %fusion.14.own_ref), custom_call_target="tpu_custom_call" | custom-call | tf_op jit(solution)/shard_map/gather_rows/pallas_call | solution.py:146
  183.1 45.3 %run_experts.1 = (bf16[32,8,16,2048]{3,2,1,0:T(8,128)(2,1)}, bf16[32,128,128]{2,1,0:T(8,128)(2,1)}) custom-call(s32[1]{0:T(128)} %bitcast.17.first_ref, bf16[32,128,2048]{2,1,0:T(8,128)(2,1)} %gather_rows.1.rows_ref, bf16[32,16,128]{2,1,0:T(8,128)(2,1)} %bitcast.100, bf16[8,2048,352]{2,1,0:T(8,128)(2,1)} %copy.83.gate_ref, ...), custom_call_target="tpu_custom_call" | custom-call | tf_op jit(solution)/shard_map/run_experts/pallas_call | solution.py:495
  228.5 114.7 %combine_rows.1 = f32[128,2048]{1,0:T(8,128)} custom-call(bf16[32,128,128]{2,1,0:T(8,128)(2,1)} %get-tuple-element.8.combiner_ref, bf16[32,128,2048]{2,1,0:T(8,128)(2,1)} %bitcast.92), custom_call_target="tpu_custom_call" | custom-call | tf_op jit(solution)/shard_map/combine_rows/pallas_call | solution.py:335
  343.2 2.1 fusion.15
  (19 shorter events, 0.1 us)
Async XLA Ops:
  0.6 7.1 %copy-start = (bf16[512,512]{1,0:T(8,128)(2,1)S(1)}, bf16[512,512]{1,0:T(8,128)(2,1)}, u32[]{:S(2)}) copy-start(bf16[512,512]{1,0:T(8,128)(2,1)} %param.14) | copy-start | bytes 1572868
  4.9 35.3 %copy-start.5 = (bf16[512,512]{1,0:T(8,128)(2,1)S(1)}, bf16[512,512]{1,0:T(8,128)(2,1)}, u32[]{:S(2)}) copy-start(bf16[512,512]{1,0:T(8,128)(2,1)} %param.12) | copy-start | bytes 1572868
  48.4 34.8 %all-to-all-start = ((bf16[4,128,512]{2,1,0:T(8,128)(2,1)}), bf16[4,128,512]{2,1,0:T(8,128)(2,1)S(1)}, u32[]{:S(2)}, u32[]{:S(2)}) async-start(bf16[4,128,512]{2,1,0:T(8,128)(2,1)} %all_to_all.14), calls=%async_computation | async-start | bytes 1048576 | tf_op jit(solution)/shard_map/all_to_all | solution.py:648
  67.7 15.8 %copy-start.3 = (bf16[128,2048]{1,0:T(8,128)(2,1)S(1)}, bf16[128,2048]{1,0:T(8,128)(2,1)}, u32[]{:S(2)}) copy-start(bf16[128,2048]{1,0:T(8,128)(2,1)} %param.16) | copy-start | bytes 1572868
  83.5 4.8 %copy-start.4 = (f32[2048]{0:T(1024)S(1)}, f32[2048]{0:T(1024)}, u32[]{:S(2)}) copy-start(f32[2048]{0:T(1024)} %param.18) | copy-start | bytes 24580
  88.2 254.9 %copy-start.2 = (bf16[128,2048]{1,0:T(8,128)(2,1)}, bf16[128,2048]{1,0:T(8,128)(2,1)S(1)}, u32[]{:S(2)}) copy-start(bf16[128,2048]{1,0:T(8,128)(2,1)S(1)} %get-tuple-element.19) | copy-start | bytes 1572868
  228.5 116.8 %copy-start.1 = (bf16[512,512]{1,0:T(8,128)(2,1)S(1)}, bf16[512,512]{1,0:T(8,128)(2,1)}, u32[]{:S(2)}) copy-start(bf16[512,512]{1,0:T(8,128)(2,1)} %param.14) | copy-start | bytes 1572868

commit v3 on v2

--- a/solution.py
+++ b/solution.py
@@ -55,7 +55,7 @@
     at.meet()
     sends = []
 
-    def send(src, dst, sem, to):
+    def send(src, dst, sem, to, when):
         copy = pltpu.make_async_remote_copy(
             src_ref=src,
             dst_ref=dst,
@@ -64,8 +64,11 @@
             device_id=to,
             device_id_type=MESH,
         )
-        copy.start()
-        sends.append(copy)
+        sends.append((when, copy))
+        if when is None:
+            copy.start()
+        else:
+            pl.when(when)(copy.start)
 
     def rows_of(z, x, y, c, h):
         block = out_ref.at[block_at(z, x, y, c)]
@@ -74,18 +77,14 @@
     def sem_of(sems, z, x, y, h):
         return sems.at[((z * 2 + x) * 2 + y) * 2 + (0 if h is None else h)]
 
-    def forward(z, x, y, h, to, src=None):
+    def forward(z, x, y, h, to, when=None, src=None):
         ref = rows_of(z, x, y, at.c, h)
-        send(ref if src is None else src, ref, sem_of(recv_sem, z, x, y, h), to)
+        send(ref if src is None else src, ref, sem_of(recv_sem, z, x, y, h), to, when)
 
     def forward_core(z, x, y, h, src=None):
         ref = rows_of(z, x, y, at.c, h)
-        send(
-            ref if src is None else src,
-            ref,
-            sem_of(core_sem, z, x, y, h),
-            device(at.z, at.x, at.y, at.fc),
-        )
+        to = device(at.z, at.x, at.y, at.fc)
+        send(ref if src is None else src, ref, sem_of(core_sem, z, x, y, h), to, None)
 
     def arrive(sems, z, x, y, c, h):
         ref = rows_of(z, x, y, c, h)
@@ -93,23 +92,37 @@
 
     local = pltpu.make_async_copy(own_ref, out_ref.at[block_at(at.z, at.x, at.y, at.c)], local_sem)
     local.start()
-    for dz in range(1, nz):
-        forward(at.z, at.x, at.y, None, device(at.turn(dz), at.x, at.y, at.c), own_ref)
-
     to_x = device(at.z, at.fx, at.y, at.c)
     to_y = device(at.z, at.x, at.fy, at.c)
-
-    def column(dz):
-        z = at.turn(dz)
-        if dz:
-            arrive(recv_sem, z, at.x, at.y, at.c, None)
-        src = None if dz else own_ref
-        forward(z, at.x, at.y, None, to_x, src)
-        forward(z, at.x, at.y, None, to_y, src)
+    to_up = device(jnp.minimum(at.z + 1, nz - 1), at.x, at.y, at.c)
+    to_down = device(jnp.maximum(at.z - 1, 0), at.x, at.y, at.c)
+    more_up, more_down = at.z < nz - 1, at.z > 0
+
+    def spread(z, src=None):
+        forward(z, at.x, at.y, None, to_x, None, src)
+        forward(z, at.x, at.y, None, to_y, None, src)
         forward_core(z, at.x, at.y, None, src)
 
-    def turned(dz):
-        z = at.turn(dz)
+    forward(at.z, at.x, at.y, None, to_up, more_up, own_ref)
+    forward(at.z, at.x, at.y, None, to_down, more_down, own_ref)
+    spread(at.z, own_ref)
+
+    def nearest(k):
+        reach = jnp.minimum(at.z, nz - 1 - at.z)
+        both = k < 2 * reach
+        far = k - reach + 1
+        low = jnp.where(both, k % 2 == 0, at.z > reach)
+        distance = jnp.where(both, k // 2 + 1, far)
+        return jnp.where(low, at.z - distance, at.z + distance), low
+
+    def column(k):
+        z, low = nearest(k)
+        arrive(recv_sem, z, at.x, at.y, at.c, None)
+        forward(z, at.x, at.y, None, to_up, low & more_up)
+        forward(z, at.x, at.y, None, to_down, jnp.logical_not(low) & more_down)
+        spread(z)
+
+    def turned(z):
         arrive(recv_sem, z, at.fx, at.y, at.c, None)
         forward(z, at.fx, at.y, 0, to_y)
         forward_core(z, at.fx, at.y, None)
@@ -117,26 +130,28 @@
         forward(z, at.x, at.fy, 1, to_x)
         forward_core(z, at.x, at.fy, None)
 
-    order = [0] + [d for k in range(1, nz) for d in sorted({k, nz - k}) if k <= nz - k]
-    column(order[0])
-    for before, now in zip(order, order[1:]):
-        column(now)
-        turned(before)
-    turned(order[-1])
-    for dz in order:
-        z = at.turn(dz)
+    column(0)
+    turned(at.z)
+    for k in range(1, nz - 1):
+        column(k)
+    for k in range(nz - 1):
+        turned(nearest(k)[0])
+    order = [at.z] + [nearest(k)[0] for k in range(nz - 1)]
+    for z in order:
         for h in range(2):
             arrive(recv_sem, z, at.fx, at.fy, at.c, h)
             forward_core(z, at.fx, at.fy, h)
-    for dz in order:
-        z = at.turn(dz)
+    for z in order:
         arrive(core_sem, z, at.x, at.y, at.fc, None)
         arrive(core_sem, z, at.fx, at.y, at.fc, None)
         arrive(core_sem, z, at.x, at.fy, at.fc, None)
         arrive(core_sem, z, at.fx, at.fy, at.fc, 0)
         arrive(core_sem, z, at.fx, at.fy, at.fc, 1)
-    for copy in sends:
-        copy.wait_send()
+    for when, copy in sends:
+        if when is None:
+            copy.wait_send()
+        else:
+            pl.when(when)(copy.wait_send)
     local.wait()
 
 
@@ -179,7 +194,12 @@
     at = Grid(nz)
     rows = acc.shape[1]
     half = rows // 2
-    spots = [(z, x, y) for x, y in ((1, 1), (1, 0), (0, 1), (0, 0)) for z in range(1, nz + 1)]
+    lead = 1
+    spots = []
+    for z in range(1, nz + 2 * lead + 1):
+        spots += [(z, 1, 1)] if z <= nz else []
+        spots += [(z - lead, 1, 0), (z - lead, 0, 1)] if 1 <= z - lead <= nz else []
+        spots += [(z - 2 * lead, 0, 0)] if z > 2 * lead else []
     sends = []
 
     def where(spot):
@@ -472,11 +492,12 @@
     def _():
         e = step - waves
         total = x_ref.shape[1]
-        part = min(total, 256)
+        part = min(total, 512)
         for p in range(0, total, part):
             x = x_ref[e, p : p + part, :]
-            gate = jnp.dot(x, gate_ref[0], preferred_element_type=jnp.float32)
-            up = jnp.dot(x, up_ref[0], preferred_element_type=jnp.float32)
+            across = (((1,), (1,)), ((), ()))
+            gate = lax.dot_general(x, gate_ref[0], across, preferred_element_type=jnp.float32)
+            up = lax.dot_general(x, up_ref[0], across, preferred_element_type=jnp.float32)
             hidden = (jax.nn.silu(gate) * up).astype(jnp.bfloat16)
             made = jnp.dot(hidden, down_ref[0], preferred_element_type=jnp.float32)
             out_ref[p // slots : (p + part) // slots, 0] = made.astype(jnp.bfloat16).reshape(
@@ -503,8 +524,8 @@
             pl.BlockSpec(memory_space=pltpu.SMEM),
             pl.BlockSpec((count, rows, width), wave),
             pl.BlockSpec((count,) + routes.shape[1:], wave),
-            pl.BlockSpec((1, width, units), turn),
-            pl.BlockSpec((1, width, units), turn),
+            pl.BlockSpec((1, units, width), turn),
+            pl.BlockSpec((1, units, width), turn),
             pl.BlockSpec((1, units, width), turn),
         ],
         out_specs=(
@@ -516,7 +537,14 @@
             dimension_semantics=("arbitrary",), vmem_limit_bytes=56 * 1024 * 1024
         ),
         name="run_experts",
-    )(first, all_rows, routes, gate_proj, up_proj, down_proj)
+    )(
+        first,
+        all_rows,
+        routes,
+        jnp.swapaxes(gate_proj, 1, 2),
+        jnp.swapaxes(up_proj, 1, 2),
+        down_proj,
+    )
     return out.reshape(blocks, experts * slots, width), mix
 
 

time: 347 us -> 278 us (0.80)
  Pallas kernels: 282 us -> 239 us
  local copies, waits for them, and re-layouts: 36.6 us -> 4.7 us
  blocking collectives: 0 us -> 11.2 us
  starting transfers between devices: 3.65 us -> 0 us
    unnamed x18 -> x16, local copies, waits for them, and re-layouts: 31.5 us -> 0.37 us
    pallas_call x1, Pallas kernels: 115 us -> 87.2 us  [combine_rows(): pl.pallas_call(functools.partial(combine_kernel, nz), out_shape=jax.Shape...]
    pallas_call x1, Pallas kernels: 93.9 us -> 79.6 us  [gather_rows(): pl.pallas_call(functools.partial(gather_kernel, nz), out_shape=jax.ShapeD...]
    all_to_all x0 -> x1, blocking collectives: none -> 11.2 us  [on_device(): lax.all_to_all(mixed_rows, 'grp', split_axis=0, concat_axis=1, tiled=True)]
    all_to_all x1 -> x0, starting transfers between devices: 3.65 us -> none  [on_device(): lax.all_to_all(mixed_rows, 'grp', split_axis=0, concat_axis=1, tiled=True)]
  transfers between devices with their start and end apart: 1 -> 0, of which waited for: 0 -> 0; matrix products, arithmetic and copies ran while one was open for 9% -> 0% of each run, Pallas kernels for 0% -> 0%
where the time goes in v3:
time: 278 us
  Pallas kernels  239 us (86%)
  matrix products  11.7 us (4%)
  blocking collectives  11.2 us (4%)
  other arithmetic  10.2 us (4%)
  local copies, waits for them, and re-layouts  4.7 us (2%)
    pallas_call x1, Pallas kernels, combine_rows(): pl.pallas_call(functools.partial(combine_kernel, nz), out_shape=jax.Shape...  87.2 us
    pallas_call x1, Pallas kernels, gather_rows(): pl.pallas_call(functools.partial(gather_kernel, nz), out_shape=jax.ShapeD...  79.6 us
    pallas_call x1, Pallas kernels, run_experts(): pl.pallas_call(functools.partial(expert_kernel, waves, slots), grid=(wave...  43.8 us
    pallas_call x1, Pallas kernels, share(): pl.pallas_call(functools.partial(share_kernel, nz), out_shape=(jax.ShapeD...  28.4 us
    all_to_all x1, blocking collectives, on_device(): lax.all_to_all(mixed_rows, 'grp', split_axis=0, concat_axis=1, tiled=True)  11.2 us

profile of v3, /device:TPU:0, one launch (start us, length us, event | category | flops | bytes accessed | tf_op | source)
XLA Modules:
  0.0 277.7 jit_solution(17711558038081467962)
XLA Ops:
  0.6 0.0 copy-start
  0.7 0.8 reshape.183
  1.4 1.2 reduce-window.6
  2.6 0.2 slice_reduce_fusion
  2.8 0.2 reduce-window.9
  3.0 0.1 add_bitcast_fusion
  3.0 0.1 slice.33
  3.1 0.1 copy.82
  3.2 0.1 iota_compare_fusion
  3.3 0.7 convert_element_type.120
  4.0 0.7 convert_element_type.121
  4.7 0.1 exponential_bitcast_fusion.1
  4.8 0.1 mul.52
  4.9 0.0 copy-start.5
  4.9 0.3 copy.81
  5.3 1.6 multiply_reduce_fusion.1
  6.9 0.2 copy.86
  7.1 0.6 pad.8.route_ref
  7.7 0.0 copy-done
  7.7 0.3 convolution_convert_fusion
  8.0 0.1 broadcast_in_dim.87
  8.1 0.1 broadcast_in_dim.86
  8.2 0.7 fusion.45.state_ref
  8.9 28.4 %share.1 = (bf16[4,2,2,2,16,128]{5,4,3,2,1,0:T(8,128)(2,1)}, bf16[4,2,4,144,128]{4,3,2,1,0:T(8,128)(2,1)}) custom-call(bf16[16,128]{1,0:T(8,128)(2,1)} %pad.8.route_ref, bf16[4,144,128]{2,1,0:T(8,128)(2,1)} %fusion.45.state_ref), custom_call_target="tpu_custom_call" | custom-call | tf_op jit(solution)/shard_map/share/pallas_call | solution.py:434
  37.2 1.0 fusion.49
  38.2 0.1 copy.83
  38.3 0.1 copy.84
  38.4 0.1 select_reduce_fusion
  38.5 0.1 copy.71
  38.6 1.6 multiply_reduce_fusion
  40.2 1.9 fusion
  42.2 1.7 fusion.6
  43.9 1.4 fusion.22
  45.3 0.0 copy-start.3
  45.3 1.7 fusion.11
  47.0 0.4 copy.75
  47.4 0.2 all_to_all.14
  47.6 11.2 %all_to_all.19 = bf16[4,128,512]{2,1,0:T(8,128)(2,1)S(1)} all-to-all(bf16[4,128,512]{2,1,0:T(8,128)(2,1)S(1)} %all_to_all.14), channel_id=1, replica_groups=mesh['ctx'=8,'grp'=4] {'grp'}, dimensions={0} | all-to-all | bytes 1048576 | tf_op jit(solution)/shard_map/all_to_all | solution.py:676
  58.8 0.3 copy.76
  59.1 0.0 copy-done.3
  59.1 0.0 copy-start.4
  59.1 4.8 %fusion.12 = (f32[128]{0:T(128)S(1)}, bf16[128,2048]{1,0:T(8,128)(2,1)S(1)}) fusion(bf16[128,2048]{0,1:T(8,128)(2,1)S(1)} %bitcast.98, bf16[2048,2048]{1,0:T(8,128)(2,1)} %param.17, bf16[128,2048]{1,0:T(8,128)(2,1)S(1)} %copy-done.3), kind=kOutput, calls=%fused_computation.21 | convolution fusion | flops 1075314560 | bytes 9961984 | tf_op jit(solution)/shard_map/dot_general | solution.py:677
  63.9 0.0 copy-start.2
  63.9 1.0 fusion.14.own_ref
  64.9 79.6 %gather_rows.1.rows_ref = bf16[32,128,2048]{2,1,0:T(8,128)(2,1)} custom-call(bf16[128,2048]{1,0:T(8,128)(2,1)} %fusion.14.own_ref), custom_call_target="tpu_custom_call" | custom-call | tf_op jit(solution)/shard_map/gather_rows/pallas_call | solution.py:161
  144.6 43.8 %run_experts.1 = (bf16[32,8,16,2048]{3,2,1,0:T(8,128)(2,1)}, bf16[32,128,128]{2,1,0:T(8,128)(2,1)}) custom-call(s32[1]{0:T(128)} %bitcast.17.first_ref, bf16[32,128,2048]{2,1,0:T(8,128)(2,1)} %gather_rows.1.rows_ref, bf16[32,16,128]{2,1,0:T(8,128)(2,1)} %bitcast.104, bf16[8,352,2048]{2,1,0:T(8,128)(2,1)} %bitcast.95, bf16[8,352,2048]{2,1,0:T(8,128)(2,1)} %bitcast.96, ...), custom_call_target="tpu_custom_call" | custom-call | tf_op jit(solution)/shard_map/run_experts/pallas_call | solution.py:516
  188.4 87.2 %combine_rows.1 = f32[128,2048]{1,0:T(8,128)} custom-call(bf16[32,128,128]{2,1,0:T(8,128)(2,1)} %get-tuple-element.8.combiner_ref, bf16[32,128,2048]{2,1,0:T(8,128)(2,1)} %bitcast.94), custom_call_target="tpu_custom_call" | custom-call | tf_op jit(solution)/shard_map/combine_rows/pallas_call | solution.py:355
  275.6 2.1 fusion.15
  (16 shorter events, 0.1 us)
Async XLA Ops:
  0.6 7.1 %copy-start = (bf16[512,512]{1,0:T(8,128)(2,1)S(1)}, bf16[512,512]{1,0:T(8,128)(2,1)}, u32[]{:S(2)}) copy-start(bf16[512,512]{1,0:T(8,128)(2,1)} %param.14) | copy-start | bytes 1572868
  4.9 35.3 %copy-start.5 = (bf16[512,512]{1,0:T(8,128)(2,1)S(1)}, bf16[512,512]{1,0:T(8,128)(2,1)}, u32[]{:S(2)}) copy-start(bf16[512,512]{1,0:T(8,128)(2,1)} %param.12) | copy-start | bytes 1572868
  45.3 13.8 %copy-start.3 = (bf16[128,2048]{1,0:T(8,128)(2,1)S(1)}, bf16[128,2048]{1,0:T(8,128)(2,1)}, u32[]{:S(2)}) copy-start(bf16[128,2048]{1,0:T(8,128)(2,1)} %param.16) | copy-start | bytes 1572868
  59.1 4.8 %copy-start.4 = (f32[2048]{0:T(1024)S(1)}, f32[2048]{0:T(1024)}, u32[]{:S(2)}) copy-start(f32[2048]{0:T(1024)} %param.18) | copy-start | bytes 24580
  63.9 211.7 %copy-start.2 = (bf16[128,2048]{1,0:T(8,128)(2,1)}, bf16[128,2048]{1,0:T(8,128)(2,1)S(1)}, u32[]{:S(2)}) copy-start(bf16[128,2048]{1,0:T(8,128)(2,1)S(1)} %get-tuple-element.19) | copy-start | bytes 1572868
  188.4 89.4 %copy-start.1 = (bf16[512,512]{1,0:T(8,128)(2,1)S(1)}, bf16[512,512]{1,0:T(8,128)(2,1)}, u32[]{:S(2)}) copy-start(bf16[512,512]{1,0:T(8,128)(2,1)} %param.14) | copy-start | bytes 1572868

commit v4 on v3

--- a/solution.py
+++ b/solution.py
@@ -49,9 +49,24 @@
     return (z * 2 + x) * 4 + y * 2 + c
 
 
-def gather_kernel(nz, own_ref, out_ref, send_sem, recv_sem, core_sem, local_sem):
+def gather_kernel(
+    nz,
+    own_ref,
+    routes_ref,
+    x_out,
+    mix_ref,
+    out_ref,
+    stage,
+    stage_sem,
+    send_sem,
+    recv_sem,
+    core_sem,
+    local_sem,
+):
     at = Grid(nz)
-    half = own_ref.shape[0] // 2
+    rows, width = own_ref.shape
+    half = rows // 2
+    experts, slots = stage.shape[1], stage.shape[2]
     at.meet()
     sends = []
 
@@ -130,48 +145,127 @@
         forward(z, at.x, at.fy, 1, to_x)
         forward_core(z, at.x, at.fy, None)
 
+    row = lax.broadcasted_iota(jnp.int32, (rows, rows), 0)
+    col = lax.broadcasted_iota(jnp.int32, (rows, rows), 1)
+    before = (row < col).astype(jnp.bfloat16)
+    ctx = lax.axis_index("ctx")
+    own = (lax.broadcasted_iota(jnp.int32, (experts, rows), 0) + ctx * experts).astype(jnp.float32)
+    spot = lax.broadcasted_iota(jnp.int32, (experts, slots, rows), 1).astype(jnp.float32)
+    drains = []
+
+    def dispatch(z, x, y, c):
+        b = block_at(z, x, y, c)
+        turn = len(drains) % 2
+        if len(drains) >= 2:
+            drains[-2].wait()
+        info = routes_ref[b].astype(jnp.float32)
+        hits = jnp.zeros((experts, rows), jnp.float32)
+        gates = jnp.zeros((experts, rows), jnp.float32)
+        for k in range(TOPK):
+            same = info[k : k + 1, :] == own
+            hits = jnp.where(same, 1.0, hits)
+            gates = jnp.where(same, info[TOPK + k : TOPK + k + 1, :], gates)
+        slot = jnp.dot(hits.astype(jnp.bfloat16), before, preferred_element_type=jnp.float32)
+        slot = jnp.where(hits > 0, slot, -1.0)
+        placed = jnp.where(slot[:, None, :] == spot, 1.0, 0.0)
+        weighed = (placed * gates[:, None, :]).reshape(experts * slots, rows)
+        mix_ref[b] = weighed.T.astype(jnp.bfloat16)
+        placed = placed.reshape(experts * slots, rows).astype(jnp.bfloat16)
+
+        @pl.loop(0, width // 512)
+        def _(k):
+            cols = pl.ds(pl.multiple_of(k * 512, 512), 512)
+            picked = jnp.dot(placed, out_ref[b, :, cols], preferred_element_type=jnp.float32)
+            stage[turn, :, :, cols] = picked.astype(stage.dtype).reshape(experts, slots, 512)
+
+        start = pl.multiple_of(b * slots, slots)
+        copy = pltpu.make_async_copy(
+            stage.at[turn], x_out.at[:, pl.ds(start, slots), :], stage_sem.at[turn]
+        )
+        copy.start()
+        drains.append(copy)
+
+    ready, late = [], []
+
+    def work(count, *blocks):
+        late.append(blocks)
+        ready.extend((spot, False) for spot in blocks)
+        if len(late) > 2:
+            ready.extend((spot, True) for spot in late.pop(0))
+        for _ in range(min(count, len(ready))):
+            (z, x, y, parts), other = ready.pop(0)
+            if other:
+                for h in parts:
+                    arrive(core_sem, z, x, y, at.fc, h)
+            dispatch(z, x, y, at.fc if other else at.c)
+
+    local.wait()
     column(0)
+    near = [at.z] + [nearest(k)[0] for k in range(nz - 1)]
+    work(1, (near[0], at.x, at.y, (None,)))
     turned(at.z)
+    work(
+        1,
+        (near[1], at.x, at.y, (None,)),
+        (near[0], at.fx, at.y, (None,)),
+        (near[0], at.x, at.fy, (None,)),
+    )
     for k in range(1, nz - 1):
         column(k)
-    for k in range(nz - 1):
-        turned(nearest(k)[0])
-    order = [at.z] + [nearest(k)[0] for k in range(nz - 1)]
-    for z in order:
+        work(2, (near[k + 1], at.x, at.y, (None,)))
+    for z in near[1:]:
+        turned(z)
+        work(2, (z, at.fx, at.y, (None,)), (z, at.x, at.fy, (None,)))
+    for z in near:
         for h in range(2):
             arrive(recv_sem, z, at.fx, at.fy, at.c, h)
             forward_core(z, at.fx, at.fy, h)
-    for z in order:
-        arrive(core_sem, z, at.x, at.y, at.fc, None)
-        arrive(core_sem, z, at.fx, at.y, at.fc, None)
-        arrive(core_sem, z, at.x, at.fy, at.fc, None)
-        arrive(core_sem, z, at.fx, at.fy, at.fc, 0)
-        arrive(core_sem, z, at.fx, at.fy, at.fc, 1)
+        work(3, (z, at.fx, at.fy, (0, 1)))
+    while late:
+        ready.extend((spot, True) for spot in late.pop(0))
+    while ready:
+        (z, x, y, parts), other = ready.pop(0)
+        if other:
+            for h in parts:
+                arrive(core_sem, z, x, y, at.fc, h)
+        dispatch(z, x, y, at.fc if other else at.c)
+    for copy in drains[-2:]:
+        copy.wait()
     for when, copy in sends:
         if when is None:
             copy.wait_send()
         else:
             pl.when(when)(copy.wait_send)
-    local.wait()
-
-
-def gather_rows(own, nz):
+
+
+def gather_rows(own, routes, experts, slots, nz):
     rows, width = own.shape
     blocks = nz * 8
     return pl.pallas_call(
         functools.partial(gather_kernel, nz),
-        out_shape=jax.ShapeDtypeStruct((blocks, rows, width), own.dtype),
-        in_specs=[pl.BlockSpec(memory_space=pltpu.VMEM)],
-        out_specs=pl.BlockSpec(memory_space=pl.ANY),
+        out_shape=(
+            jax.ShapeDtypeStruct((experts, blocks * slots, width), own.dtype),
+            jax.ShapeDtypeStruct((blocks, rows, experts * slots), own.dtype),
+        ),
+        in_specs=[pl.BlockSpec(memory_space=pltpu.VMEM)] * 2,
+        out_specs=(
+            pl.BlockSpec(memory_space=pl.ANY),
+            pl.BlockSpec(memory_space=pltpu.VMEM),
+        ),
         scratch_shapes=[
+            pltpu.VMEM((blocks, rows, width), own.dtype),
+            pltpu.VMEM((2, experts, slots, width), own.dtype),
+            pltpu.SemaphoreType.DMA((2,)),
             pltpu.SemaphoreType.DMA((nz * 16,)),
             pltpu.SemaphoreType.DMA((nz * 8,)),
             pltpu.SemaphoreType.DMA((nz * 8,)),
             pltpu.SemaphoreType.DMA,
         ],
-        compiler_params=pltpu.CompilerParams(collective_id=0, has_side_effects=True),
+        compiler_params=pltpu.CompilerParams(
+            collective_id=0, has_side_effects=True, vmem_limit_bytes=40 * 1024 * 1024
+        ),
         name="gather_rows",
-    )(own)
+    )(own, routes)
 
 
 def combine_kernel(
@@ -452,100 +546,43 @@
     return routes.reshape((nz * 8,) + route.shape), states.reshape((nz * 2,) + state.shape)
 
 
-def expert_kernel(
-    waves, slots, first_ref, rows_ref, routes_ref, gate_ref, up_ref, down_ref, out_ref, mix_ref, x_ref
-):
-    step = pl.program_id(0)
-    experts = x_ref.shape[0]
-    count, rows = rows_ref.shape[0], rows_ref.shape[1]
-
-    @pl.when(step < waves)
-    def _():
-        row = lax.broadcasted_iota(jnp.int32, (rows, rows), 0)
-        col = lax.broadcasted_iota(jnp.int32, (rows, rows), 1)
-        before = (row < col).astype(jnp.bfloat16)
-        own = (
-            lax.broadcasted_iota(jnp.int32, (experts, rows), 0) + first_ref[0] * experts
-        ).astype(jnp.float32)
-        spot = lax.broadcasted_iota(jnp.int32, (experts, slots, rows), 1).astype(jnp.float32)
-        for b in range(count):
-            info = routes_ref[b].astype(jnp.float32)
-            hits = jnp.zeros((experts, rows), jnp.float32)
-            gates = jnp.zeros((experts, rows), jnp.float32)
-            for k in range(TOPK):
-                same = info[k : k + 1, :] == own
-                hits = jnp.where(same, 1.0, hits)
-                gates = jnp.where(same, info[TOPK + k : TOPK + k + 1, :], gates)
-            slot = jnp.dot(hits.astype(jnp.bfloat16), before, preferred_element_type=jnp.float32)
-            slot = jnp.where(hits > 0, slot, -1.0)
-            placed = jnp.where(slot[:, None, :] == spot, 1.0, 0.0)
-            weighed = (placed * gates[:, None, :]).reshape(experts * slots, rows)
-            mix_ref[b] = weighed.T.astype(jnp.bfloat16)
-            placed = placed.reshape(experts * slots, rows).astype(jnp.bfloat16)
-            picked = jnp.dot(placed, rows_ref[b], preferred_element_type=jnp.float32)
-            picked = picked.astype(jnp.bfloat16)
-            start = pl.multiple_of((step * count + b) * slots, slots)
-            for e in range(experts):
-                x_ref[e, pl.ds(start, slots), :] = picked[e * slots : (e + 1) * slots]
-
-    @pl.when(step >= waves)
-    def _():
-        e = step - waves
-        total = x_ref.shape[1]
-        part = min(total, 512)
-        for p in range(0, total, part):
-            x = x_ref[e, p : p + part, :]
-            across = (((1,), (1,)), ((), ()))
-            gate = lax.dot_general(x, gate_ref[0], across, preferred_element_type=jnp.float32)
-            up = lax.dot_general(x, up_ref[0], across, preferred_element_type=jnp.float32)
-            hidden = (jax.nn.silu(gate) * up).astype(jnp.bfloat16)
-            made = jnp.dot(hidden, down_ref[0], preferred_element_type=jnp.float32)
-            out_ref[p // slots : (p + part) // slots, 0] = made.astype(jnp.bfloat16).reshape(
-                part // slots, slots, made.shape[1]
-            )
-
-
-def run_experts(all_rows, routes, gate_proj, up_proj, down_proj, slots):
-    blocks, rows, width = all_rows.shape
-    experts, _, units = gate_proj.shape
-    count = 4
-    waves = blocks // count
-    first = lax.axis_index("ctx").astype(jnp.int32).reshape(1)
-    wave = lambda i: (jnp.minimum(i, waves - 1), 0, 0)
-    turn = lambda i: (jnp.maximum(i - waves, 0), 0, 0)
-    out, mix = pl.pallas_call(
-        functools.partial(expert_kernel, waves, slots),
-        grid=(waves + experts,),
-        out_shape=(
-            jax.ShapeDtypeStruct((blocks, experts, slots, width), jnp.bfloat16),
-            jax.ShapeDtypeStruct((blocks, rows, experts * slots), jnp.bfloat16),
-        ),
+def expert_kernel(slots, x_ref, gate_ref, up_ref, down_ref, out_ref):
+    total = x_ref.shape[1]
+    part = min(total, 512)
+    across = (((1,), (1,)), ((), ()))
+    for p in range(0, total, part):
+        x = x_ref[0, p : p + part, :]
+        gate = lax.dot_general(x, gate_ref[0], across, preferred_element_type=jnp.float32)
+        up = lax.dot_general(x, up_ref[0], across, preferred_element_type=jnp.float32)
+        hidden = (jax.nn.silu(gate) * up).astype(jnp.bfloat16)
+        made = jnp.dot(hidden, down_ref[0], preferred_element_type=jnp.float32)
+        out_ref[p // slots : (p + part) // slots, 0] = made.astype(jnp.bfloat16).reshape(
+            part // slots, slots, made.shape[1]
+        )
+
+
+def run_experts(picked, gate_proj, up_proj, down_proj, slots):
+    experts, total, width = picked.shape
+    units = gate_proj.shape[2]
+    blocks = total // slots
+    turn = lambda e: (e, 0, 0)
+    out = pl.pallas_call(
+        functools.partial(expert_kernel, slots),
+        grid=(experts,),
+        out_shape=jax.ShapeDtypeStruct((blocks, experts, slots, width), jnp.bfloat16),
         in_specs=[
-            pl.BlockSpec(memory_space=pltpu.SMEM),
-            pl.BlockSpec((count, rows, width), wave),
-            pl.BlockSpec((count,) + routes.shape[1:], wave),
+            pl.BlockSpec((1, total, width), turn),
             pl.BlockSpec((1, units, width), turn),
             pl.BlockSpec((1, units, width), turn),
             pl.BlockSpec((1, units, width), turn),
         ],
-        out_specs=(
-            pl.BlockSpec((blocks, 1, slots, width), lambda i: (0, jnp.maximum(i - waves, 0), 0, 0)),
-            pl.BlockSpec((count, rows, experts * slots), wave),
-        ),
-        scratch_shapes=[pltpu.VMEM((experts, blocks * slots, width), jnp.bfloat16)],
+        out_specs=pl.BlockSpec((blocks, 1, slots, width), lambda e: (0, e, 0, 0)),
         compiler_params=pltpu.CompilerParams(
-            dimension_semantics=("arbitrary",), vmem_limit_bytes=56 * 1024 * 1024
+            dimension_semantics=("arbitrary",), vmem_limit_bytes=40 * 1024 * 1024
         ),
         name="run_experts",
-    )(
-        first,
-        all_rows,
-        routes,
-        jnp.swapaxes(gate_proj, 1, 2),
-        jnp.swapaxes(up_proj, 1, 2),
-        down_proj,
-    )
-    return out.reshape(blocks, experts * slots, width), mix
+    )(picked, jnp.swapaxes(gate_proj, 1, 2), jnp.swapaxes(up_proj, 1, 2), down_proj)
+    return out.reshape(blocks, experts * slots, width)
 
 
 def pack_route(expert_ids, gate_weights):
@@ -684,10 +721,8 @@
     capacity = (5 * row_count * TOPK + 4 * E - 1) // (4 * E)
     capacity = (capacity + 15) // 16 * 16
     if kernels:
-        all_rows = gather_rows(normed, nz)
-        partial_rows, combiner = run_experts(
-            all_rows, routes, gate_proj, up_proj, down_proj, capacity
-        )
+        picked, combiner = gather_rows(normed, routes, local_experts, capacity, nz)
+        partial_rows = run_experts(picked, gate_proj, up_proj, down_proj, capacity)
         expert_mix = combine_rows(combiner, partial_rows, nz)
     else:
         all_ids = lax.all_gather(expert_ids, everyone, axis=0, tiled=True)

time: 278 us -> 277 us (level)
  Pallas kernels: 239 us -> 232 us
  local copies, waits for them, and re-layouts: 4.7 us -> 9.83 us
    pallas_call x2, Pallas kernels: 123 us -> 118 us  [the longest x1 86.8 us: gather_rows(): pl.pallas_call(functools.partial(gather_kernel, nz), out_shape=(jax.Shape...]
    all_to_all x2, local copies, waits for them, and re-layouts: 0.47 us -> 4.22 us  [on_device(): lax.all_to_all(mixed_rows, 'grp', split_axis=0, concat_axis=1, tiled=True)]
where the time goes in v4:
time: 277 us
  Pallas kernels  232 us (84%)
  blocking collectives  13 us (5%)
  matrix products  12.1 us (4%)
  local copies, waits for them, and re-layouts  9.83 us (4%)
  other arithmetic  9.37 us (3%)
    pallas_call x1, Pallas kernels, gather_rows(): pl.pallas_call(functools.partial(gather_kernel, nz), out_shape=(jax.Shape...  86.8 us
    pallas_call x1, Pallas kernels, combine_rows(): pl.pallas_call(functools.partial(combine_kernel, nz), out_shape=jax.Shape...  84.8 us
    pallas_call x1, Pallas kernels, run_experts(): pl.pallas_call(functools.partial(expert_kernel, slots), grid=(experts,),...  31.7 us
    pallas_call x1, Pallas kernels, share(): pl.pallas_call(functools.partial(share_kernel, nz), out_shape=(jax.ShapeD...  28.4 us
    all_to_all x1, blocking collectives, on_device(): lax.all_to_all(mixed_rows, 'grp', split_axis=0, concat_axis=1, tiled=True)  13 us

profile of v4, /device:TPU:0, one launch (start us, length us, event | category | flops | bytes accessed | tf_op | source)
XLA Modules:
  0.0 276.9 jit_solution(119847442250845010)
XLA Ops:
  0.6 0.0 copy-start
  0.7 0.8 reshape.180
  1.4 1.2 reduce-window.6
  2.6 0.2 slice_reduce_fusion
  2.8 0.2 reduce-window.9
  3.0 0.1 add_bitcast_fusion
  3.0 0.1 slice.33
  3.1 0.1 copy.82
  3.2 0.1 iota_compare_fusion
  3.3 0.7 convert_element_type.120
  4.0 0.7 convert_element_type.121
  4.7 0.1 exponential_bitcast_fusion.1
  4.8 0.1 mul.52
  4.9 0.0 copy-start.7
  4.9 0.3 copy.81
  5.3 1.6 multiply_reduce_fusion.1
  6.9 0.2 copy.86
  7.1 0.6 pad.8.route_ref
  7.7 0.3 convolution_convert_fusion
  8.0 0.1 broadcast_in_dim.87
  8.1 0.1 broadcast_in_dim.86
  8.2 0.7 fusion.45.state_ref
  8.9 28.4 %share.1 = (bf16[4,2,2,2,16,128]{5,4,3,2,1,0:T(8,128)(2,1)}, bf16[4,2,4,144,128]{4,3,2,1,0:T(8,128)(2,1)}) custom-call(bf16[16,128]{1,0:T(8,128)(2,1)} %pad.8.route_ref, bf16[4,144,128]{2,1,0:T(8,128)(2,1)} %fusion.45.state_ref), custom_call_target="tpu_custom_call" | custom-call | tf_op jit(solution)/shard_map/share/pallas_call | solution.py:528
  37.3 1.0 fusion.49
  38.2 0.1 copy.83
  38.3 0.1 copy.84
  38.5 0.1 select_reduce_fusion
  38.6 0.1 copy.71
  38.6 1.6 multiply_reduce_fusion
  40.3 0.0 copy-done.7
  40.3 1.9 fusion
  42.2 1.7 fusion.6
  43.9 1.4 fusion.22
  45.3 1.7 fusion.11
  47.0 1.2 copy.75
  48.2 2.2 all_to_all.14
  50.4 13.0 %all_to_all.19 = bf16[4,128,512]{2,1,0:T(8,128)(2,1)} all-to-all(bf16[4,128,512]{2,1,0:T(8,128)(2,1)} %all_to_all.14), channel_id=1, replica_groups=mesh['ctx'=8,'grp'=4] {'grp'}, dimensions={0} | all-to-all | bytes 1048576 | tf_op jit(solution)/shard_map/all_to_all | solution.py:713
  63.5 2.0 copy.76
  65.5 5.1 %fusion.12 = (f32[128]{0:T(128)S(1)}, bf16[128,2048]{1,0:T(8,128)(2,1)S(1)}) fusion(bf16[128,2048]{0,1:T(8,128)(2,1)} %bitcast.100, bf16[2048,2048]{1,0:T(8,128)(2,1)} %param.17, bf16[128,2048]{1,0:T(8,128)(2,1)} %param.16), kind=kOutput, calls=%fused_computation.21 | convolution fusion | flops 1075314560 | bytes 9961984 | tf_op jit(solution)/shard_map/dot_general | solution.py:714
  70.6 0.0 copy-start.4
  70.6 0.0 copy-done.6
  70.6 0.2 fusion.14.own_ref
  70.8 0.6 copy-done.4
  71.4 86.8 %gather_rows.1 = (bf16[8,512,2048]{2,1,0:T(8,128)(2,1)}, bf16[32,128,128]{2,1,0:T(8,128)(2,1)S(1)}) custom-call(bf16[128,2048]{1,0:T(8,128)(2,1)S(1)} %fusion.14.own_ref, bf16[32,16,128]{2,1,0:T(8,128)(2,1)S(1)} %bitcast.96), custom_call_target="tpu_custom_call" | custom-call | tf_op jit(solution)/shard_map/gather_rows/pallas_call | solution.py:244
  158.3 31.7 %run_experts.1 = bf16[32,8,16,2048]{3,2,1,0:T(8,128)(2,1)} custom-call(bf16[8,512,2048]{2,1,0:T(8,128)(2,1)} %get-tuple-element.9.x_ref, bf16[8,352,2048]{2,1,0:T(8,128)(2,1)S(1)} %bitcast.95, bf16[8,352,2048]{2,1,0:T(8,128)(2,1)} %bitcast.98, bf16[8,352,2048]{2,1,0:T(8,128)(2,1)} %down_ref.1), custom_call_target="tpu_custom_call" | custom-call | tf_op jit(solution)/shard_map/run_experts/pallas_call | solution.py:569
  189.9 0.0 copy-done.2
  190.0 84.8 %combine_rows.1 = f32[128,2048]{1,0:T(8,128)} custom-call(bf16[32,128,128]{2,1,0:T(8,128)(2,1)} %copy-done.2, bf16[32,128,2048]{2,1,0:T(8,128)(2,1)} %bitcast.97), custom_call_target="tpu_custom_call" | custom-call | tf_op jit(solution)/shard_map/combine_rows/pallas_call | solution.py:449
  274.7 2.1 fusion.15
  (27 shorter events, 0.1 us)
Async XLA Ops:
  0.6 7.1 %copy-start = (bf16[512,512]{1,0:T(8,128)(2,1)S(1)}, bf16[512,512]{1,0:T(8,128)(2,1)}, u32[]{:S(2)}) copy-start(bf16[512,512]{1,0:T(8,128)(2,1)} %param.14) | copy-start | bytes 1572868
  4.9 35.3 %copy-start.7 = (bf16[512,512]{1,0:T(8,128)(2,1)S(1)}, bf16[512,512]{1,0:T(8,128)(2,1)}, u32[]{:S(2)}) copy-start(bf16[512,512]{1,0:T(8,128)(2,1)} %param.12) | copy-start | bytes 1572868
  48.2 110.0 %slice-start = ((s8[11534336]{0:T(1024)(128)(4,1)}), s8[3145728]{0:T(1024)(128)(4,1)S(1)}, s32[]{:S(2)}) async-start(s8[11534336]{0:T(1024)(128)(4,1)} %bitcast.93), calls=%async_computation.1 | async-start | bytes 6291456
  65.5 5.1 %copy-start.6 = (f32[2048]{0:T(1024)S(1)}, f32[2048]{0:T(1024)}, u32[]{:S(2)}) copy-start(f32[2048]{0:T(1024)} %param.18) | copy-start | bytes 24580
  65.5 5.9 %copy-start.3 = (bf16[4,2,2,2,16,128]{5,4,3,2,1,0:T(8,128)(2,1)S(1)}, bf16[4,2,2,2,16,128]{5,4,3,2,1,0:T(8,128)(2,1)}, u32[]{:S(2)}) copy-start(bf16[4,2,2,2,16,128]{5,4,3,2,1,0:T(8,128)(2,1)} %get-tuple-element.7) | copy-start | bytes 393220
  65.5 92.7 %slice-start.1 = ((s8[11534336]{0:T(1024)(128)(4,1)}), s8[4194304]{0:T(1024)(128)(4,1)S(1)}, s32[]{:S(2)}) async-start(s8[11534336]{0:T(1024)(128)(4,1)} %bitcast.93), calls=%async_computation.2 | async-start | bytes 8388608
  65.5 92.7 %slice-start.2 = ((s8[11534336]{0:T(1024)(128)(4,1)}), s8[4194304]{0:T(1024)(128)(4,1)S(1)}, s32[]{:S(2)}) async-start(s8[11534336]{0:T(1024)(128)(4,1)} %bitcast.93), calls=%async_computation.3 | async-start | bytes 8388608
  70.6 0.8 copy-start.4
  158.2 31.7 %copy-start.2 = (bf16[32,128,128]{2,1,0:T(8,128)(2,1)}, bf16[32,128,128]{2,1,0:T(8,128)(2,1)S(1)}, u32[]{:S(2)}) copy-start(bf16[32,128,128]{2,1,0:T(8,128)(2,1)S(1)} %get-tuple-element.8.combiner_ref) | copy-start | bytes 3145732
  189.9 84.8 %copy-start.5 = (bf16[128,2048]{1,0:T(8,128)(2,1)S(1)}, bf16[128,2048]{1,0:T(8,128)(2,1)}, u32[]{:S(2)}) copy-start(bf16[128,2048]{1,0:T(8,128)(2,1)} %copy-done.4) | copy-start | bytes 1572868
  189.9 86.9 %copy-start.1 = (bf16[512,512]{1,0:T(8,128)(2,1)S(1)}, bf16[512,512]{1,0:T(8,128)(2,1)}, u32[]{:S(2)}) copy-start(bf16[512,512]{1,0:T(8,128)(2,1)} %param.14) | copy-start | bytes 1572868

commit v5 on v4

--- a/solution.py
+++ b/solution.py
@@ -471,6 +471,57 @@
     )(combiner, outs)
 
 
+def swap_kernel(count, mixed_ref, out_ref, send_sem, recv_sem):
+    ctx, grp = lax.axis_index("ctx"), lax.axis_index("grp")
+    rows, width = out_ref.shape[0], mixed_ref.shape[1]
+    barrier = pltpu.get_barrier_semaphore()
+    others = [lax.rem(grp + d, count) for d in range(1, count)]
+    for other in others:
+        pl.semaphore_signal(barrier, inc=1, device_id=(ctx, other), device_id_type=MESH)
+    pl.semaphore_wait(barrier, count - 1)
+
+    def rows_for(g):
+        return pl.ds(pl.multiple_of(g * rows, rows), rows)
+
+    def heads_of(g):
+        return pl.ds(pl.multiple_of(g * width, width), width)
+
+    sends = []
+    for d, other in enumerate(others):
+        copy = pltpu.make_async_remote_copy(
+            src_ref=mixed_ref.at[rows_for(other)],
+            dst_ref=out_ref.at[:, heads_of(grp)],
+            send_sem=send_sem.at[d],
+            recv_sem=recv_sem.at[grp],
+            device_id=(ctx, other),
+            device_id_type=MESH,
+        )
+        copy.start()
+        sends.append(copy)
+    out_ref[:, heads_of(grp)] = mixed_ref[rows_for(grp), :]
+    for other in others:
+        ref = out_ref.at[:, heads_of(other)]
+        pltpu.make_async_copy(ref, ref, recv_sem.at[other]).wait()
+    for copy in sends:
+        copy.wait_send()
+
+
+def swap_heads(mixed, count):
+    rows, width = mixed.shape
+    return pl.pallas_call(
+        functools.partial(swap_kernel, count),
+        out_shape=jax.ShapeDtypeStruct((rows // count, width * count), mixed.dtype),
+        in_specs=[pl.BlockSpec(memory_space=pltpu.VMEM)],
+        out_specs=pl.BlockSpec(memory_space=pltpu.VMEM),
+        scratch_shapes=[
+            pltpu.SemaphoreType.DMA((count - 1,)),
+            pltpu.SemaphoreType.DMA((count,)),
+        ],
+        compiler_params=pltpu.CompilerParams(collective_id=3, has_side_effects=True),
+        name="swap_heads",
+    )(mixed)
+
+
 def share_kernel(
     nz, route_ref, state_ref, routes_ref, states_ref, send_sem, z_sem, x_sem, small_sem, far_sem
 ):
@@ -710,7 +761,10 @@
     mixed_rows = block_output(
         feat_query, feat_key, value_rows, cumulative, preceding_state, prior_norm
     )
-    head_rows = lax.all_to_all(mixed_rows, "grp", split_axis=0, concat_axis=1, tiled=True)
+    if kernels:
+        head_rows = swap_heads(mixed_rows, lax.axis_size("grp"))
+    else:
+        head_rows = lax.all_to_all(mixed_rows, "grp", split_axis=0, concat_axis=1, tiled=True)
     projected = jnp.dot(head_rows, out_weight, preferred_element_type=jnp.float32)
     attended = (residual.astype(jnp.float32) + projected).astype(jnp.bfloat16)
     widened = attended.astype(jnp.float32)

time: 277 us -> 275 us (level)
  blocking collectives: 13 us -> 0 us
  Pallas kernels: 232 us -> 244 us
  local copies, waits for them, and re-layouts: 9.83 us -> 6.62 us
    all_to_all x1 -> x0, blocking collectives: 13 us -> none  [on_device(): lax.all_to_all(mixed_rows, 'grp', split_axis=0, concat_axis=1, tiled=True)]
    pallas_call x0 -> x1, Pallas kernels: none -> 8.61 us  [swap_heads(): pl.pallas_call(functools.partial(swap_kernel, count), out_shape=jax.Shape...]
    all_to_all x2 -> x0, local copies, waits for them, and re-layouts: 4.22 us -> none  [on_device(): lax.all_to_all(mixed_rows, 'grp', split_axis=0, concat_axis=1, tiled=True)]
    pallas_call x1, Pallas kernels: 86.8 us -> 90.8 us  [gather_rows(): pl.pallas_call(functools.partial(gather_kernel, nz), out_shape=(jax.Shape...]
where the time goes in v5:
time: 275 us
  Pallas kernels  244 us (89%)
  matrix products  13.7 us (5%)
  other arithmetic  9.42 us (3%)
  local copies, waits for them, and re-layouts  6.62 us (2%)
    pallas_call x1, Pallas kernels, gather_rows(): pl.pallas_call(functools.partial(gather_kernel, nz), out_shape=(jax.Shape...  90.8 us
    pallas_call x1, Pallas kernels, combine_rows(): pl.pallas_call(functools.partial(combine_kernel, nz), out_shape=jax.Shape...  84.5 us
    pallas_call x1, Pallas kernels, run_experts(): pl.pallas_call(functools.partial(expert_kernel, slots), grid=(experts,),...  31.7 us
    pallas_call x1, Pallas kernels, share(): pl.pallas_call(functools.partial(share_kernel, nz), out_shape=(jax.ShapeD...  28.4 us
    pallas_call x1, Pallas kernels, swap_heads(): pl.pallas_call(functools.partial(swap_kernel, count), out_shape=jax.Shape...  8.61 us

profile of v5, /device:TPU:0, one launch (start us, length us, event | category | flops | bytes accessed | tf_op | source)
XLA Modules:
  0.0 274.7 jit_solution(15904366109596665937)
XLA Ops:
  0.6 0.0 copy-start
  0.7 0.7 convert_element_type.120
  1.4 0.7 convert_element_type.121
  2.1 0.6 pad.8.route_ref
  2.7 0.7 reshape.178
  3.4 1.2 reduce-window.6
  4.6 0.2 slice_reduce_fusion
  4.8 0.2 reduce-window.9
  5.0 0.1 add_bitcast_fusion
  5.1 0.1 slice.33
  5.1 0.1 copy.76
  5.2 0.1 broadcast_in_dim.87
  5.3 0.1 broadcast_in_dim.86
  5.4 0.1 exponential_bitcast_fusion.1
  5.5 0.1 iota_compare_fusion
  5.6 0.1 mul.52
  5.7 0.3 copy.74
  6.0 1.6 multiply_reduce_fusion.1
  7.7 0.2 copy.80
  7.9 0.3 convolution_convert_fusion
  8.2 0.7 fusion.45.state_ref
  8.9 28.4 %share.1 = (bf16[4,2,2,2,16,128]{5,4,3,2,1,0:T(8,128)(2,1)}, bf16[4,2,4,144,128]{4,3,2,1,0:T(8,128)(2,1)}) custom-call(bf16[16,128]{1,0:T(8,128)(2,1)} %pad.8.route_ref, bf16[4,144,128]{2,1,0:T(8,128)(2,1)} %fusion.45.state_ref), custom_call_target="tpu_custom_call" | custom-call | tf_op jit(solution)/shard_map/share/pallas_call | solution.py:579
  37.3 1.0 fusion.49
  38.2 0.1 copy.77
  38.3 0.1 copy.78
  38.5 0.1 select_reduce_fusion
  38.6 0.1 copy.67
  38.6 1.6 multiply_reduce_fusion
  40.3 2.4 fusion.22
  42.7 1.9 fusion
  44.7 0.0 copy-start.8
  44.7 1.4 fusion.6
  46.1 0.0 slice-start
  46.1 2.5 fusion.11
  48.6 2.0 copy.75.mixed_ref
  50.6 8.6 %swap_heads.1 = bf16[128,2048]{1,0:T(8,128)(2,1)} custom-call(bf16[512,512]{1,0:T(8,128)(2,1)} %copy.75.mixed_ref), custom_call_target="tpu_custom_call" | custom-call | tf_op jit(solution)/shard_map/swap_heads/pallas_call | solution.py:511
  59.2 0.0 copy-start.6
  59.2 0.0 slice-start.1
  59.3 0.0 slice-start.2
  59.3 5.1 %fusion.12 = (f32[128]{0:T(128)S(1)}, bf16[128,2048]{1,0:T(8,128)(2,1)S(1)}) fusion(bf16[128,2048]{1,0:T(8,128)(2,1)} %swap_heads.1, bf16[2048,2048]{1,0:T(8,128)(2,1)} %param.17, bf16[128,2048]{1,0:T(8,128)(2,1)} %param.16), kind=kOutput, calls=%fused_computation.21 | convolution fusion | flops 1075314560 | bytes 9961984 | tf_op jit(solution)/shard_map/dot_general | solution.py:768
  64.4 0.0 copy-start.4
  64.4 0.8 copy-done.4
  65.2 0.0 copy-done.6
  65.2 0.2 fusion.14.own_ref
  65.4 90.8 %gather_rows.1 = (bf16[8,512,2048]{2,1,0:T(8,128)(2,1)}, bf16[32,128,128]{2,1,0:T(8,128)(2,1)S(1)}) custom-call(bf16[128,2048]{1,0:T(8,128)(2,1)S(1)} %fusion.14.own_ref, bf16[32,16,128]{2,1,0:T(8,128)(2,1)S(1)} %bitcast.95), custom_call_target="tpu_custom_call" | custom-call | tf_op jit(solution)/shard_map/gather_rows/pallas_call | solution.py:244
  156.3 31.7 %run_experts.1 = bf16[32,8,16,2048]{3,2,1,0:T(8,128)(2,1)} custom-call(bf16[8,512,2048]{2,1,0:T(8,128)(2,1)} %get-tuple-element.9.x_ref, bf16[8,352,2048]{2,1,0:T(8,128)(2,1)S(1)} %bitcast.94, bf16[8,352,2048]{2,1,0:T(8,128)(2,1)} %bitcast.97, bf16[8,352,2048]{2,1,0:T(8,128)(2,1)} %down_ref.1), custom_call_target="tpu_custom_call" | custom-call | tf_op jit(solution)/shard_map/run_experts/pallas_call | solution.py:620
  188.0 84.5 %combine_rows.1 = f32[128,2048]{1,0:T(8,128)} custom-call(bf16[32,128,128]{2,1,0:T(8,128)(2,1)} %copy-done.2, bf16[32,128,2048]{2,1,0:T(8,128)(2,1)} %bitcast.96), custom_call_target="tpu_custom_call" | custom-call | tf_op jit(solution)/shard_map/combine_rows/pallas_call | solution.py:449
  272.5 2.1 fusion.15
  (27 shorter events, 0.1 us)
Async XLA Ops:
  0.6 7.2 %copy-start = (bf16[512,512]{1,0:T(8,128)(2,1)S(1)}, bf16[512,512]{1,0:T(8,128)(2,1)}, u32[]{:S(2)}) copy-start(bf16[512,512]{1,0:T(8,128)(2,1)} %param.14) | copy-start | bytes 1572868
  7.6 35.1 %copy-start.7 = (bf16[512,512]{1,0:T(8,128)(2,1)S(1)}, bf16[512,512]{1,0:T(8,128)(2,1)}, u32[]{:S(2)}) copy-start(bf16[512,512]{1,0:T(8,128)(2,1)} %param.12) | copy-start | bytes 1572868
  44.7 1.4 copy-start.8
  46.1 110.2 %slice-start = ((s8[11534336]{0:T(1024)(128)(4,1)}), s8[3145728]{0:T(1024)(128)(4,1)S(1)}, s32[]{:S(2)}) async-start(s8[11534336]{0:T(1024)(128)(4,1)} %bitcast.92), calls=%async_computation | async-start | bytes 6291456
  59.2 6.0 %copy-start.6 = (f32[2048]{0:T(1024)S(1)}, f32[2048]{0:T(1024)}, u32[]{:S(2)}) copy-start(f32[2048]{0:T(1024)} %param.18) | copy-start | bytes 24580
  59.2 6.2 %copy-start.3 = (bf16[4,2,2,2,16,128]{5,4,3,2,1,0:T(8,128)(2,1)S(1)}, bf16[4,2,2,2,16,128]{5,4,3,2,1,0:T(8,128)(2,1)}, u32[]{:S(2)}) copy-start(bf16[4,2,2,2,16,128]{5,4,3,2,1,0:T(8,128)(2,1)} %get-tuple-element.7) | copy-start | bytes 393220
  59.2 97.0 %slice-start.1 = ((s8[11534336]{0:T(1024)(128)(4,1)}), s8[4194304]{0:T(1024)(128)(4,1)S(1)}, s32[]{:S(2)}) async-start(s8[11534336]{0:T(1024)(128)(4,1)} %bitcast.92), calls=%async_computation.1 | async-start | bytes 8388608
  59.3 97.0 %slice-start.2 = ((s8[11534336]{0:T(1024)(128)(4,1)}), s8[4194304]{0:T(1024)(128)(4,1)S(1)}, s32[]{:S(2)}) async-start(s8[11534336]{0:T(1024)(128)(4,1)} %bitcast.92), calls=%async_computation.2 | async-start | bytes 8388608
  64.4 0.8 copy-start.4
  156.3 31.7 %copy-start.2 = (bf16[32,128,128]{2,1,0:T(8,128)(2,1)}, bf16[32,128,128]{2,1,0:T(8,128)(2,1)S(1)}, u32[]{:S(2)}) copy-start(bf16[32,128,128]{2,1,0:T(8,128)(2,1)S(1)} %get-tuple-element.8.combiner_ref) | copy-start | bytes 3145732
  188.0 84.5 %copy-start.5 = (bf16[128,2048]{1,0:T(8,128)(2,1)S(1)}, bf16[128,2048]{1,0:T(8,128)(2,1)}, u32[]{:S(2)}) copy-start(bf16[128,2048]{1,0:T(8,128)(2,1)} %copy-done.4) | copy-start | bytes 1572868
  188.0 86.7 %copy-start.1 = (bf16[512,512]{1,0:T(8,128)(2,1)S(1)}, bf16[512,512]{1,0:T(8,128)(2,1)}, u32[]{:S(2)}) copy-start(bf16[512,512]{1,0:T(8,128)(2,1)} %param.14) | copy-start | bytes 1572868
